TPU v7x, 512 devices: a whole 4x8x8 slice. The times are simulated.
512 devices in a mesh: rows: 8 (over z), ctx: 64 (over x, y, core).
Axes of the slice: x: 4, y: 8, z: 8, core: 2. Of those that a mesh axis runs over, the one named last changes fastest.
Arguments:
- nope_query: bfloat16 [8, 2, 128, 128], P('rows', None, 'ctx'), may hold values from -6 to 6
- rope_query: bfloat16 [8, 2, 128, 64], P('rows', None, 'ctx'), may hold values from -6 to 6
- key_lift: bfloat16 [128, 128, 512], P('ctx'), may hold values from -2 to 2
- value_lift: bfloat16 [128, 512, 128], P('ctx'), may hold values from -0.25 to 0.25
- out_weight: bfloat16 [16384, 7168], P('ctx', 'rows'), may hold values from -0.125 to 0.125
- latent_cache: bfloat16 [8, 65536, 576], P('rows', 'ctx'), may hold values from -100 to 100
- lengths: int32 [8], P('rows'), may hold values from 2 to 65536, as said below
Outputs:
- layer_out: float32 [8, 2, 7168], P(None, None, ('rows', 'ctx'))
Inputs may be any that keep to these rules, and one draw needn't show every extreme that they name: `lengths`: in every draw one sequence has exactly 65536 cached positions.
All inputs are finite; a program needn't handle non-finite values.
Results may differ from a plain program's by a relative error of at most 0.0099.
Values may be sent and summed in bfloat16 or wider, within the bound.
A program may use at most 128 MiB of HBM per device.

v0:
```python
import jax
import jax.numpy as jnp
from jax import lax
from jax.sharding import PartitionSpec as P

DN = 128
DR = 64
LAT = 512
DV = 128


def combined_all(shard, axis, combine):
    everything = jax.tree.map(lambda part: lax.all_gather(part, axis), shard)
    first = jax.tree.map(lambda part: part[0], everything)

    def lap(k, so_far):
        return combine(so_far, jax.tree.map(lambda part: part[k], everything))

    return lax.fori_loop(1, lax.axis_size(axis), lap, first)


def combine_partials(earlier, later):
    max_early, sum_early, out_early = earlier
    max_late, sum_late, out_late = later
    joined_max = jnp.maximum(max_early, max_late)
    factor_early = jnp.exp(max_early - joined_max)
    factor_late = jnp.exp(max_late - joined_max)
    joined_sum = sum_early * factor_early + sum_late * factor_late
    joined_out = out_early * factor_early[..., None] + out_late * factor_late[..., None]
    return (joined_max, joined_sum, joined_out)


def on_device(nope_query, rope_query, key_lift, value_lift, out_weight, latent_cache, lengths):
    new_tokens = nope_query.shape[1]
    heads_here = nope_query.shape[2]
    latent_query = jnp.einsum(
        "qhn,hnl->qhl", nope_query[0], key_lift, preferred_element_type=jnp.float32
    ).astype(jnp.bfloat16)
    local_query = jnp.concatenate([latent_query, rope_query[0]], axis=-1)
    every_query = lax.all_gather(local_query, "ctx", axis=1, tiled=True)
    heads_all = every_query.shape[1]
    width = every_query.shape[2]
    row_count = new_tokens * heads_all
    query_rows = every_query.reshape(row_count, width)
    latent_rows = latent_cache[0]
    length = lengths[0]
    key_span = 512
    block_count = latent_rows.shape[0] // key_span
    first_position = lax.axis_index("ctx") * latent_rows.shape[0]
    score_scale = (DN + DR) ** (-0.5)
    visible_end = length - new_tokens + 1 + jnp.arange(row_count, dtype=jnp.int32) // heads_all

    def advance(block_index, carry):
        running_max, running_sum, running_out = carry
        start = block_index * key_span
        key_block = lax.dynamic_slice_in_dim(latent_rows, start, key_span, 0)
        scores = (
            jnp.einsum("rd,kd->rk", query_rows, key_block, preferred_element_type=jnp.float32)
            * score_scale
        )
        positions = first_position + start + jnp.arange(key_span, dtype=jnp.int32)
        visible = positions[None, :] < visible_end[:, None]
        new_max = jnp.maximum(running_max, jnp.max(jnp.where(visible, scores, -1e30), axis=1))
        shrink = jnp.exp(running_max - new_max)
        expo = jnp.where(visible, jnp.exp(scores - new_max[:, None]), 0.0)
        running_sum = running_sum * shrink + jnp.sum(expo, axis=1)
        running_out = running_out * shrink[:, None] + jnp.dot(
            expo.astype(jnp.bfloat16), key_block[:, :LAT], preferred_element_type=jnp.float32
        )
        return (new_max, running_sum, running_out)

    start_carry = (
        jnp.full((row_count,), -1e30, jnp.float32),
        jnp.zeros((row_count,), jnp.float32),
        jnp.zeros((row_count, LAT), jnp.float32),
    )
    running_max, running_sum, running_out = lax.fori_loop(0, block_count, advance, start_carry)
    running_max = running_max.reshape(new_tokens, heads_all)
    running_sum = running_sum.reshape(new_tokens, heads_all)
    running_out = running_out.reshape(new_tokens, heads_all, LAT)
    joined_max, joined_sum, joined_out = combined_all(
        (running_max, running_sum, running_out), "ctx", combine_partials
    )
    head_start = lax.axis_index("ctx") * heads_here
    own_sum = lax.dynamic_slice_in_dim(joined_sum, head_start, heads_here, 1)
    own_out = lax.dynamic_slice_in_dim(joined_out, head_start, heads_here, 1)
    head_out = jnp.einsum(
        "qhl,hlv->qhv",
        (own_out / own_sum[..., None]).astype(jnp.bfloat16),
        value_lift,
        preferred_element_type=jnp.float32,
    ).astype(jnp.bfloat16)
    flattened = head_out.reshape(1, new_tokens, heads_here * DV)
    every_sequence = lax.all_gather(flattened, "rows", axis=0, tiled=True)
    sequence_count = every_sequence.shape[0]
    partial_sums = jnp.dot(
        every_sequence.reshape(sequence_count * new_tokens, heads_here * DV),
        out_weight,
        preferred_element_type=jnp.float32,
    )
    summed = lax.psum_scatter(partial_sums, "ctx", scatter_dimension=1, tiled=True)
    return summed.reshape(sequence_count, new_tokens, summed.shape[1])


def solution(mesh):
    in_specs = (
        P("rows", None, "ctx", None),
        P("rows", None, "ctx", None),
        P("ctx", None, None),
        P("ctx", None, None),
        P("ctx", "rows"),
        P("rows", "ctx", None),
        P("rows"),
    )
    out_specs = P(None, None, ("rows", "ctx"))
    return jax.shard_map(
        on_device, mesh=mesh, in_specs=in_specs, out_specs=out_specs, check_vma=False
    )
```

profile of v0, /device:TPU:1, one launch (start us, length us, event | category | flops | bytes accessed | tf_op | source)
XLA Modules:
  0.0 557.0 jit_solution(1497243127908036249)
XLA Ops:
  6.6 1.8 copy.18
  8.6 50.3 %all_gather.15 = bf16[2,128,576]{2,0,1:T(2,128)(2,1)S(1)} all-gather(bf16[2,2,576]{2,0,1:T(2,128)(2,1)S(1)} %pad_maximum_fusion), channel_id=1, replica_groups=mesh['rows'=8,'ctx'=64] {'ctx'}, dimensions={1}, use_global_device_ids=true | all-gather | bytes 299520 | tf_op jit(solution)/shard_map/all_gather | solution.py:40
  59.6 2.3 while.38
  62.8 1.3 dynamic-slice
  64.9 37.9 %all_gather.17 = f32[64,2,128]{2,1,0:T(2,128)S(1)} all-gather(f32[1,2,128]{2,1,0:T(2,128)S(1)} %bitcast.58), channel_id=1, replica_groups=mesh['rows'=8,'ctx'=64] {'ctx'}, dimensions={0}, use_global_device_ids=true | all-gather | bytes 66560 | tf_op jit(solution)/shard_map/all_gather | solution.py:13
  102.7 36.5 %all_gather.16 = f32[64,2,128]{2,1,0:T(2,128)S(1)} all-gather(f32[1,2,128]{2,1,0:T(2,128)S(1)} %bitcast.57), channel_id=1, replica_groups=mesh['rows'=8,'ctx'=64] {'ctx'}, dimensions={0}, use_global_device_ids=true | all-gather | bytes 66560 | tf_op jit(solution)/shard_map/all_gather | solution.py:13
  139.2 70.9 %all-gather.2.cloned.1.call-done = f32[64,2,128,512]{3,2,1,0:T(8,128)} async-done(((f32[1,2,128,512]{3,2,1,0:T(8,128)}), f32[64,2,128,512]{3,2,1,0:T(8,128)}) %all-gather.2.cloned.1.call-update) | async-done | bytes 33554448 | tf_op jit(solution)/shard_map/all_gather | solution.py:13
  211.2 79.7 %while.37 = (s32[]{:T(128)}, f32[2,128]{1,0:T(2,128)S(1)}, f32[2,128]{1,0:T(2,128)S(1)}, f32[2,128,512]{2,1,0:T(8,128)S(1)}, f32[64,2,128]{2,1,0:T(2,128)S(1)}, ...) while((s32[]{:T(128)}, f32[2,128]{1,0:T(2,128)S(1)}, ...), condition=%wide.region_5.6_spmd, body=%wide.region_4.5_spmd.sunk | while | flops 394757 | bytes 1583255 | solution.py:19
  211.2 1.2 fusion.45
  212.5 1.2 fusion.45
  213.8 1.2 fusion.45
  215.1 1.2 fusion.45
  216.3 1.2 fusion.45
  220.1 1.2 fusion.45
  221.4 1.2 fusion.45
  222.7 1.2 fusion.45
  223.9 1.2 fusion.45
  229.0 1.2 fusion.45
  230.3 1.2 fusion.45
  231.5 1.2 fusion.45
  232.8 1.2 fusion.45
  236.6 1.2 fusion.45
  237.9 1.2 fusion.45
  239.1 1.2 fusion.45
  240.4 1.2 fusion.45
  244.2 1.2 fusion.45
  245.4 1.2 fusion.45
  246.7 1.2 fusion.45
  248.0 1.2 fusion.45
  253.0 1.2 fusion.45
  291.3 13.6 %all_gather.19 = bf16[8,2,256]{2,1,0:T(2,128)(2,1)S(1)} all-gather(bf16[1,2,256]{2,1,0:T(2,128)(2,1)S(1)} %fusion.23), channel_id=1, replica_groups=mesh['rows'=8,'ctx'=64] {'rows'}, dimensions={0}, use_global_device_ids=true | all-gather | bytes 9216 | tf_op jit(solution)/shard_map/all_gather | solution.py:94
  305.1 244.4 %all-reduce = f32[16,896]{1,0:T(8,128)S(1)} all-reduce(f32[16,896]{1,0:T(8,128)S(1)} %fusion.28), channel_id=2, replica_groups=mesh['rows'=8,'ctx'=64] {'ctx'}, use_global_device_ids=true, to_apply=%region_6.7.clone | all-reduce | flops 14336 | bytes 114688
  (150 shorter events, 56.8 us)
Async XLA Ops:
  6.5 298.4 %copy-start = (bf16[256,896]{1,0:T(8,128)(2,1)S(1)}, bf16[256,896]{1,0:T(8,128)(2,1)}, u32[]{:S(2)}) copy-start(bf16[256,896]{1,0:T(8,128)(2,1)} %param.15) | copy-start | bytes 1376260
  6.5 1.9 copy-start.5
  6.5 1.9 copy-start.4
  6.5 1.9 copy-start.2
  6.5 203.6 %all-gather.2.cloned.1.call-start = ((), (), s32[]{:S(2)}) async-start(), calls=%async_computation | async-start | bytes 34078720 | tf_op jit(solution)/shard_map/all_gather | solution.py:13
  62.0 0.8 copy-start.1
  211.2 79.9 %copy-start.3 = (bf16[2,512,128]{2,1,0:T(8,128)(2,1)S(1)}, bf16[2,512,128]{2,1,0:T(8,128)(2,1)}, u32[]{:S(2)}) copy-start(bf16[2,512,128]{2,1,0:T(8,128)(2,1)} %param.14) | copy-start | bytes 786436
Sparse Core Ops, SparseCore 0:
  62.9 147.1 all-gather.1
where the time goes:
time: 562 us; the launch traced here: 557 us
  blocking collectives  383 us (68%)
  other arithmetic  78.4 us (14%)
  waiting for transfers between devices  70.9 us (13%)
  between operations  14.9 us (3%)
  local copies, waits for them, and re-layouts  5.82 us (1%)
    unnamed x1, blocking collectives  244 us
    add x63, other arithmetic, combine_partials(): out_early * factor_early[..., None] + out_late * factor_late[..., None]  76.3 us
    all_gather x2, blocking collectives, combined_all(): everything = jax.tree.map(lambda part: lax.all_gather(part, axis), shard)  74.4 us
    all_gather x1, waiting for transfers between devices, combined_all(): everything = jax.tree.map(lambda part: lax.all_gather(part, axis), shard)  70.9 us
    all_gather x1, blocking collectives, on_device(): every_query = lax.all_gather(local_query, 'ctx', axis=1, tiled=True)  50.3 us
    all_gather x1, blocking collectives, on_device(): every_sequence = lax.all_gather(flattened, 'rows', axis=0, tiled=True)  13.6 us
  transfers between devices with their start and end apart: 1, of which 1 were waited for; matrix products, arithmetic and copies ran while one was open for 0% of the time, Pallas kernels for 0%

commit v1 on v0

v1 whole, which is shorter than its diff:
```python
import functools

import jax
import jax.numpy as jnp
from jax import lax
from jax.experimental import pallas as pl
from jax.experimental.pallas import tpu as pltpu
from jax.sharding import PartitionSpec as P

DN = 128
DR = 64
LAT = 512
DV = 128
X, Y, Z = 4, 8, 8
G = 2 * X
COLS = 14
LOG2E = 1.4426950408889634
LOWEST = -1e30

MESH = pl.DeviceIdType.MESH
F32 = jnp.float32
BF16 = jnp.bfloat16

AWAY = [(dx, dc) for dx in range(X) for dc in range(2)]
ROWS = 4 * Y
ROWS_BITS = ROWS.bit_length() - 1


def iota(shape, axis):
    return lax.broadcasted_iota(jnp.int32, shape, axis)


def dot(a, b):
    return jnp.dot(a, b, preferred_element_type=F32)


def farthest_first(n):
    return sorted(range(1, n), key=lambda d: -min(d, n - d))


def one_where(condition):
    return jnp.where(condition, 1.0, 0.0).astype(BF16)


def split_three(value):
    high = value.astype(BF16)
    rest = value - high.astype(F32)
    middle = rest.astype(BF16)
    low = (rest - middle.astype(F32)).astype(BF16)
    return high, middle, low


def stat_tile(value, rows):
    high, middle, low = split_three(jnp.broadcast_to(value, (rows, 128)))
    lane = iota((rows, 128), 1)
    tile = jnp.where(
        lane == 0,
        high.astype(F32),
        jnp.where(lane == 1, middle.astype(F32), jnp.where(lane == 2, low.astype(F32), 0.0)),
    )
    return tile.astype(BF16)


def read_stat(tile):
    return jnp.sum(tile.astype(F32), axis=1, keepdims=True)


def combine(parts, stats):
    top = functools.reduce(jnp.maximum, stats)
    factors = [jnp.exp2(stat - top) for stat in stats]
    weight = functools.reduce(jnp.add, factors)
    total = functools.reduce(jnp.add, [f * p for f, p in zip(factors, parts)])
    return total / weight, top + jnp.log2(weight)


def kernel(
    lengths,
    nope_hbm,
    rope_hbm,
    key_lift_hbm,
    value_lift_hbm,
    weight_hbm,
    cache_hbm,
    out,
    nope,
    rope,
    key_lift,
    value_lift,
    weight,
    cache,
    placed,
    near_q,
    all_q,
    part_out,
    part_in,
    own_out,
    own_in,
    heads,
    sums_out,
    sums_in,
    last_out,
    last_in,
    local_sem,
    send_sem,
    recv_sem,
):
    row = lax.axis_index("rows")
    ctx = lax.axis_index("ctx")
    core = ctx & 1
    y = (ctx >> 1) & (Y - 1)
    x = ctx >> Y.bit_length()

    def along_y(d):
        return (row, (x * Y + ((y + d) & (Y - 1))) * 2 + core)

    def in_group(dx, dc):
        return (row, (((x + dx) & (X - 1)) * Y + y) * 2 + ((core + dc) & 1))

    def along_z(d):
        return ((row + d) & (Z - 1), ctx)

    loads = [
        pltpu.make_async_copy(key_lift_hbm, key_lift, local_sem.at[0]),
        pltpu.make_async_copy(cache_hbm, cache.at[0, pl.ds(0, LAT + DR)], local_sem.at[1]),
        pltpu.make_async_copy(weight_hbm, weight, local_sem.at[2]),
        pltpu.make_async_copy(value_lift_hbm, value_lift, local_sem.at[3]),
        pltpu.make_async_copy(nope_hbm, nope, local_sem.at[4]),
        pltpu.make_async_copy(rope_hbm, rope, local_sem.at[5]),
    ]
    for at in (0, 4, 5):
        loads[at].start()

    barrier = pltpu.get_barrier_semaphore()
    partners = (
        [in_group(*away) for away in AWAY[1:]]
        + [along_y(d) for d in range(1, Y)]
        + [along_z(d) for d in range(1, Z)]
    )
    for partner in partners:
        pl.semaphore_signal(barrier, inc=1, device_id=partner, device_id_type=MESH)
    for at in (1, 2, 3):
        loads[at].start()

    def send(stage, slot, source, target, device):
        copy = pltpu.make_async_remote_copy(
            src_ref=source,
            dst_ref=target,
            send_sem=send_sem.at[stage, slot],
            recv_sem=recv_sem.at[stage, slot],
            device_id=device,
            device_id_type=MESH,
        )
        copy.start()
        return copy

    row16 = iota((16, 128), 0)
    even = (row16 & 1) == 0
    for at in (4, 5, 0):
        loads[at].wait()
    nope_rows = nope[0].astype(F32)
    rope_rows = rope[0].astype(F32)
    latent = jnp.zeros((16, 128), F32)
    rotary = jnp.zeros((16, DR), F32)
    for h in range(2):
        left = jnp.where(
            even,
            jnp.broadcast_to(nope_rows[0, h : h + 1, :], (16, DN)),
            jnp.broadcast_to(nope_rows[1, h : h + 1, :], (16, DN)),
        ).astype(BF16)
        lifted = dot(left, key_lift[h])
        for c in range(4):
            latent = jnp.where(
                (row16 >> 1) == 2 * c + h, lifted[:, 128 * c : 128 * (c + 1)], latent
            )
        for j in range(2):
            rotary = jnp.where(
                row16[:, :DR] == 2 * h + j,
                jnp.broadcast_to(rope_rows[j, h : h + 1, :], (16, DR)),
                rotary,
            )
    near_q[0, 0:16, :] = latent.astype(BF16)
    near_q[0, 16:32, :] = jnp.concatenate([rotary, jnp.zeros((16, 128 - DR), F32)], axis=1).astype(BF16)
    for part in range(2):
        cache[part, LAT + DR :, :] = jnp.zeros((128 - DR, cache.shape[2]), BF16)

    pl.semaphore_wait(barrier, len(partners))

    sent = [send(0, d, near_q.at[0], near_q.at[d], along_y(d)) for d in farthest_first(Y)]
    shared = send(0, 0, cache_hbm, cache.at[1, pl.ds(0, LAT + DR)], in_group(0, 1))

    r = iota((5 * ROWS, Y * 32), 0)
    k = iota((5 * ROWS, Y * 32), 1)
    i = r & (ROWS - 1)
    spread = one_where(k == (i >> 2) * 32 + (r >> ROWS_BITS) * 4 + (i & 3))
    r = iota((Y * 32, 5 * ROWS), 0)
    k = iota((Y * 32, 5 * ROWS), 1)
    place = r & 31
    gather = one_where(k == jnp.minimum(place >> 2, 4) * ROWS + (r >> 5) * 4 + (place & 3))
    for copy in sent:
        copy.wait_recv()
    rows = dot(spread, near_q[...].reshape(Y * 32, 128))
    for c in range(5):
        all_q[0, :, 128 * c : 128 * (c + 1)] = rows[ROWS * c : ROWS * (c + 1)].astype(BF16)

    last = sent
    sent = {dx: send(1, dx, all_q.at[0], all_q.at[dx], in_group(dx, 0)) for dx in farthest_first(X)}
    for copy in last:
        copy.wait_send()

    loads[2].wait()
    span = Y * 2 * COLS
    for ax in range(X):
        low = ax * span // 128 * 128
        high = min(-(-(ax + 1) * span // 128) * 128, X * span)
        n = iota((high - low, 256), 0) + low
        lane = iota((1, 256), 1)
        to_core, to_y, column = lane >> 7, (y + ((lane & 127) >> 4)) & (Y - 1), lane & 15
        source = ((ax * Y + to_y) * 2 + to_core) * COLS + column
        source = jnp.where(column < COLS, source, -1)
        choose = one_where(n == source)
        placed[:, 256 * ax : 256 * (ax + 1)] = dot(weight[:, low:high], choose).astype(BF16)

    loads[1].wait()
    span = cache.shape[2]
    count = ROWS * X
    limit = lengths[0] - 1 + (iota((count, 1), 0) & 1)
    scale = LOG2E * (DN + DR) ** -0.5
    for copy in sent.values():
        copy.wait_recv()
    query = all_q[...].reshape(count, LAT + 128)
    scores, seen = [], []
    for part in range(2):
        if part:
            shared.wait_recv()
        owner = ctx if part == 0 else ctx + 1 - 2 * core
        visible = iota((1, span), 1) + owner * span < limit
        scores.append(jnp.where(visible, dot(query, cache[part]) * scale, LOWEST))
        seen.append(visible)
    top = jnp.max(jnp.maximum(scores[0], scores[1]), axis=1, keepdims=True)
    expos = [jnp.where(v, jnp.exp2(score - top), 0.0) for v, score in zip(seen, scores)]
    denominator = jnp.maximum(jnp.sum(expos[0] + expos[1], axis=1, keepdims=True), 1e-30)
    weighted = [
        lax.dot_general(
            expo.astype(BF16), cache[part, 0:LAT, :], (((1,), (1,)), ((), ())), preferred_element_type=F32
        )
        for part, expo in enumerate(expos)
    ]
    result = ((weighted[0] + weighted[1]) / denominator).astype(BF16)
    stats = stat_tile(top + jnp.log2(denominator), count)
    part_out[:, :, 0:LAT] = result.reshape(X, ROWS, LAT)
    part_out[:, :, LAT:] = stats.reshape(X, ROWS, 128)
    back = [
        send(2, dx, part_out.at[dx], part_in.at[dx], in_group(X - dx, 0)) for dx in farthest_first(X)
    ]
    for copy in sent.values():
        copy.wait_send()
    shared.wait_send()

    loads[3].wait()
    for copy in back:
        copy.wait_recv()
    held = [part_out[0]] + [part_in[dx] for dx in range(1, X)]
    total, stat = combine(
        [part[:, 0:LAT].astype(F32) for part in held], [read_stat(part[:, LAT:]) for part in held]
    )
    total = total.astype(BF16)
    stacked = jnp.concatenate(
        [total[:, 128 * c : 128 * (c + 1)] for c in range(4)] + [stat_tile(stat, ROWS)], axis=0
    )
    own_out[...] = dot(gather, stacked).astype(BF16).reshape(Y, 32, 128)

    sent = [send(3, d, own_out.at[d], own_in.at[d], along_y(Y - d)) for d in farthest_first(Y)]
    for copy in back:
        copy.wait_send()
    r = iota((128, 16), 0)
    k = iota((128, 16), 1)
    to_row = r & 15
    block = r >> 4
    source = (block & 3) * 4 + (block >> 2) * 2 + (to_row & 1)
    pick = one_where(k == source)
    for copy in sent:
        copy.wait_recv()
    held = [own_out[0]] + [own_in[d] for d in range(1, Y)]
    latent_out, _ = combine(
        [part[0:16].astype(F32) for part in held], [read_stat(part[16:32]) for part in held]
    )
    picked = dot(pick, latent_out.astype(BF16)).astype(BF16)
    for h in range(2):
        wide = jnp.concatenate([picked[64 * h + 16 * c : 64 * h + 16 * (c + 1)] for c in range(4)], axis=1)
        heads[0, :, DV * h : DV * (h + 1)] = dot(wide, value_lift[h])[0:2].astype(BF16).astype(F32)

    last = sent
    sent = [send(4, d, heads.at[0], heads.at[d], along_z(d)) for d in farthest_first(Z)]
    for copy in last:
        copy.wait_send()
    for copy in sent:
        copy.wait_recv()
    every = jnp.concatenate([heads[d] for d in range(Z)], axis=0).astype(BF16)
    product = dot(every, placed[...])
    for g in range(G):
        sums_out[g] = product[:, 128 * g : 128 * (g + 1)]

    last = sent
    sent = []
    for g in sorted(range(1, G), key=lambda g: -min(AWAY[g][0], X - AWAY[g][0])):
        dx, dc = AWAY[g]
        chunk = ((x + dx) & (X - 1)) * 2 + ((core + dc) & 1)
        sent.append(send(5, g, sums_out.at[chunk], sums_in.at[g], in_group(dx, dc)))
    for copy in last:
        copy.wait_send()
    for copy in sent:
        copy.wait_recv()
    total = functools.reduce(jnp.add, [sums_in[g] for g in range(1, G)]) + sums_out[x * 2 + core]

    came_from = ((iota((8, 128), 1) >> 4) - iota((8, 128), 0)) & 7
    for half in range(2):
        turned = pltpu.roll(total[8 * half : 8 * half + 8], 0, 1, stride=16, stride_axis=0)
        for d in range(Y):
            line = jnp.sum(jnp.where(came_from == d, turned, 0.0), axis=0, keepdims=True)
            last_out[d, half : half + 1, :] = pltpu.roll(line, (128 - 16 * d) & 127, 1)
    last = sent
    sent = [send(6, d, last_out.at[d], last_in.at[d], along_y(d)) for d in farthest_first(Y)]
    for copy in last:
        copy.wait_send()
    for copy in sent:
        copy.wait_recv()
    total = functools.reduce(jnp.add, [last_in[d] for d in range(1, Y)]) + last_out[0]
    for half in range(2):
        wide = jnp.broadcast_to(total[half : half + 1], (8, 128))
        wide = pltpu.roll(wide, 16, 1, stride=16, stride_axis=0)
        for at in range(8):
            sequence = (row - (4 * half + at // 2)) & (Z - 1)
            out[sequence, at % 2 : at % 2 + 1, :] = wide[7 - at : 8 - at, 0:COLS]
    for copy in sent:
        copy.wait_send()


def on_device(nope_query, rope_query, key_lift, value_lift, out_weight, latent_cache, lengths):
    cache = latent_cache[0].T
    in_hbm = (nope_query, rope_query, key_lift, value_lift, out_weight, cache)
    span = cache.shape[1]
    most = max(G, Y)
    vmem = pl.BlockSpec(memory_space=pltpu.VMEM)
    hbm = pl.BlockSpec(memory_space=pltpu.HBM)
    return pl.pallas_call(
        kernel,
        out_shape=jax.ShapeDtypeStruct((Z, 2, COLS), F32),
        in_specs=[pl.BlockSpec(memory_space=pltpu.SMEM)] + [hbm] * 6,
        out_specs=vmem,
        scratch_shapes=[
            pltpu.VMEM(nope_query.shape, BF16),
            pltpu.VMEM(rope_query.shape, BF16),
            pltpu.VMEM(key_lift.shape, BF16),
            pltpu.VMEM(value_lift.shape, BF16),
            pltpu.VMEM(out_weight.shape, BF16),
            pltpu.VMEM((2, LAT + 128, span), BF16),
            pltpu.VMEM((2 * DV, 128 * G), BF16),
            pltpu.VMEM((Y, 32, 128), BF16),
            pltpu.VMEM((X, ROWS, LAT + 128), BF16),
            pltpu.VMEM((X, ROWS, LAT + 128), BF16),
            pltpu.VMEM((X, ROWS, LAT + 128), BF16),
            pltpu.VMEM((Y, 32, 128), BF16),
            pltpu.VMEM((Y, 32, 128), BF16),
            pltpu.VMEM((Z, 2, 2 * DV), F32),
            pltpu.VMEM((G, 16, 128), F32),
            pltpu.VMEM((G, 16, 128), F32),
            pltpu.VMEM((Y, 2, 128), F32),
            pltpu.VMEM((Y, 2, 128), F32),
            pltpu.SemaphoreType.DMA((6,)),
            pltpu.SemaphoreType.DMA((7, most)),
            pltpu.SemaphoreType.DMA((7, most)),
        ],
        compiler_params=pltpu.CompilerParams(
            collective_id=0, has_side_effects=True, vmem_limit_bytes=32 << 20
        ),
        cost_estimate=pl.CostEstimate(flops=600_000_000, bytes_accessed=2_500_000, transcendentals=300_000),
    )(lengths, *(pltpu.with_memory_space_constraint(a, pltpu.HBM) for a in in_hbm))


def solution(mesh):
    in_specs = (
        P("rows", None, "ctx", None),
        P("rows", None, "ctx", None),
        P("ctx", None, None),
        P("ctx", None, None),
        P("ctx", "rows"),
        P("rows", "ctx", None),
        P("rows"),
    )
    out_specs = P(None, None, ("rows", "ctx"))
    return jax.shard_map(
        on_device, mesh=mesh, in_specs=in_specs, out_specs=out_specs, check_vma=False
    )
```

time: 562 us -> 49.7 us (0.09)
  blocking collectives: 383 us -> 0 us
  other arithmetic: 78.4 us -> 0 us
  waiting for transfers between devices: 70.9 us -> 0 us
  Pallas kernels: 0 us -> 48.3 us
  between operations: 14.9 us -> 0.66 us
    unnamed x1 -> x0, blocking collectives: 244 us -> none
    all_gather x4 -> x0, blocking collectives: 138 us -> none  [the longest x2 74.4 us: combined_all(): everything = jax.tree.map(lambda part: lax.all_gather(part, axis), shard)]
    add x132 -> x0, other arithmetic: 78 us -> none  [the longest x63 76.3 us: combine_partials(): out_early * factor_early[..., None] + out_late * factor_late[..., None]]
    all_gather x1 -> x0, waiting for transfers between devices: 70.9 us -> none  [combined_all(): everything = jax.tree.map(lambda part: lax.all_gather(part, axis), shard)]
    pallas_call x0 -> x1, Pallas kernels: none -> 48.3 us  [on_device(): pl.pallas_call(kernel, out_shape=jax.ShapeDtypeStruct((Z, 2, COLS), F32),...]
  transfers between devices with their start and end apart: 1 -> 0, of which waited for: 1 -> 0; matrix products, arithmetic and copies ran while one was open for 0% -> 0% of each run, Pallas kernels for 0% -> 0%
where the time goes in v1:
time: 49.7 us; the launch traced here: 49.5 us
  Pallas kernels  48.3 us (97%)
  between operations  0.66 us (1%)
  local copies, waits for them, and re-layouts  0.6 us (1%)
    pallas_call x1, Pallas kernels, on_device(): pl.pallas_call(kernel, out_shape=jax.ShapeDtypeStruct((Z, 2, COLS), F32),...  48.3 us

profile of v1, /device:TPU:1, one launch (start us, length us, event | category | flops | bytes accessed | tf_op | source)
XLA Modules:
  0.0 49.5 jit_solution(4278691376502044239)
XLA Ops:
  0.7 48.3 %shard_map.73 = f32[8,2,14]{2,1,0:T(2,128)S(1)} custom-call(s32[1]{0:T(128)S(6)} %copy.9.lengths, bf16[1,2,2,128]{3,2,1,0:T(2,128)(2,1)} %nope_hbm.1, bf16[1,2,2,64]{3,2,1,0:T(2,128)(2,1)} %rope_hbm.1, bf16[2,128,512]{2,1,0:T(8,128)(2,1)} %key_lift_hbm.1, bf16[2,512,128]{2,1,0:T(8,128)(2,1)} %value_lift_hbm.1, bf16[256,896]{1,0:T(8,128)(2,1)} %weight_hbm.1, ...), custom_call_target="tpu_custom_call" | custom-call | flops 600000000 | bytes 2500000 | tf_op jit(solution)/shard_map/pallas_call | solution.py:345
  48.9 0.6 %copy.10 = f32[8,2,14]{2,1,0:T(2,128)} copy(f32[8,2,14]{2,1,0:T(2,128)S(1)} %shard_map.73) | data formatting | bytes 1792

commit v2 on v1

--- a/solution.py
+++ b/solution.py
@@ -63,6 +63,16 @@
 
 def read_stat(tile):
     return jnp.sum(tile.astype(F32), axis=1, keepdims=True)
+
+
+def blocks_transposed(tile):
+    row, block = iota((8, 128), 0), iota((8, 128), 1) >> 4
+    for step in (1, 2, 4):
+        above = pltpu.roll(pltpu.roll(tile, 8 - step, 0), 16 * step, 1)
+        below = pltpu.roll(pltpu.roll(tile, step, 0), 128 - 16 * step, 1)
+        stays = (row & step) == (block & step)
+        tile = jnp.where(stays, tile, jnp.where((row & step) == 0, above, below))
+    return tile
 
 
 def combine(parts, stats):
@@ -98,8 +108,6 @@
     heads,
     sums_out,
     sums_in,
-    last_out,
-    last_in,
     local_sem,
     send_sem,
     recv_sem,
@@ -141,17 +149,19 @@
     for at in (1, 2, 3):
         loads[at].start()
 
-    def send(stage, slot, source, target, device):
-        copy = pltpu.make_async_remote_copy(
+    def send(stage, source, target, device):
+        pltpu.make_async_remote_copy(
             src_ref=source,
             dst_ref=target,
-            send_sem=send_sem.at[stage, slot],
-            recv_sem=recv_sem.at[stage, slot],
+            send_sem=send_sem.at[stage],
+            recv_sem=recv_sem.at[stage],
             device_id=device,
             device_id_type=MESH,
-        )
-        copy.start()
-        return copy
+        ).start()
+
+    def wait_all(sems, stage, buffer):
+        slots = buffer.at[pl.ds(1, buffer.shape[0] - 1)]
+        pltpu.make_async_copy(slots, slots, sems.at[stage]).wait()
 
     row16 = iota((16, 128), 0)
     even = (row16 & 1) == 0
@@ -185,8 +195,10 @@
 
     pl.semaphore_wait(barrier, len(partners))
 
-    sent = [send(0, d, near_q.at[0], near_q.at[d], along_y(d)) for d in farthest_first(Y)]
-    shared = send(0, 0, cache_hbm, cache.at[1, pl.ds(0, LAT + DR)], in_group(0, 1))
+    for d in farthest_first(Y):
+        send(0, near_q.at[0], near_q.at[d], along_y(d))
+    sibling_cache = cache.at[1, pl.ds(0, LAT + DR)]
+    send(7, cache_hbm, sibling_cache, in_group(0, 1))
 
     r = iota((5 * ROWS, Y * 32), 0)
     k = iota((5 * ROWS, Y * 32), 1)
@@ -196,16 +208,14 @@
     k = iota((Y * 32, 5 * ROWS), 1)
     place = r & 31
     gather = one_where(k == jnp.minimum(place >> 2, 4) * ROWS + (r >> 5) * 4 + (place & 3))
-    for copy in sent:
-        copy.wait_recv()
+    wait_all(recv_sem, 0, near_q)
     rows = dot(spread, near_q[...].reshape(Y * 32, 128))
     for c in range(5):
         all_q[0, :, 128 * c : 128 * (c + 1)] = rows[ROWS * c : ROWS * (c + 1)].astype(BF16)
 
-    last = sent
-    sent = {dx: send(1, dx, all_q.at[0], all_q.at[dx], in_group(dx, 0)) for dx in farthest_first(X)}
-    for copy in last:
-        copy.wait_send()
+    for dx in farthest_first(X):
+        send(1, all_q.at[0], all_q.at[dx], in_group(dx, 0))
+    wait_all(send_sem, 0, near_q)
 
     loads[2].wait()
     span = Y * 2 * COLS
@@ -222,43 +232,43 @@
 
     loads[1].wait()
     span = cache.shape[2]
+    block = span // 2
     count = ROWS * X
     limit = lengths[0] - 1 + (iota((count, 1), 0) & 1)
     scale = LOG2E * (DN + DR) ** -0.5
-    for copy in sent.values():
-        copy.wait_recv()
+    wait_all(recv_sem, 1, all_q)
     query = all_q[...].reshape(count, LAT + 128)
-    scores, seen = [], []
+    tops, denominators, weighted = [], [], []
     for part in range(2):
         if part:
-            shared.wait_recv()
+            pltpu.make_async_copy(sibling_cache, sibling_cache, recv_sem.at[7]).wait()
         owner = ctx if part == 0 else ctx + 1 - 2 * core
-        visible = iota((1, span), 1) + owner * span < limit
-        scores.append(jnp.where(visible, dot(query, cache[part]) * scale, LOWEST))
-        seen.append(visible)
-    top = jnp.max(jnp.maximum(scores[0], scores[1]), axis=1, keepdims=True)
-    expos = [jnp.where(v, jnp.exp2(score - top), 0.0) for v, score in zip(seen, scores)]
-    denominator = jnp.maximum(jnp.sum(expos[0] + expos[1], axis=1, keepdims=True), 1e-30)
-    weighted = [
-        lax.dot_general(
-            expo.astype(BF16), cache[part, 0:LAT, :], (((1,), (1,)), ((), ())), preferred_element_type=F32
-        )
-        for part, expo in enumerate(expos)
-    ]
-    result = ((weighted[0] + weighted[1]) / denominator).astype(BF16)
-    stats = stat_tile(top + jnp.log2(denominator), count)
-    part_out[:, :, 0:LAT] = result.reshape(X, ROWS, LAT)
-    part_out[:, :, LAT:] = stats.reshape(X, ROWS, 128)
-    back = [
-        send(2, dx, part_out.at[dx], part_in.at[dx], in_group(X - dx, 0)) for dx in farthest_first(X)
-    ]
-    for copy in sent.values():
-        copy.wait_send()
-    shared.wait_send()
+        for start in range(0, span, block):
+            visible = iota((1, block), 1) + (owner * span + start) < limit
+            keys = cache[part, :, start : start + block]
+            scores = jnp.where(visible, dot(query, keys) * scale, LOWEST)
+            top = jnp.max(scores, axis=1, keepdims=True)
+            expo = jnp.exp2(scores - top)
+            tops.append(top)
+            denominators.append(jnp.sum(expo, axis=1, keepdims=True))
+            weighted.append(
+                lax.dot_general(
+                    expo.astype(BF16), keys[0:LAT], (((1,), (1,)), ((), ())), preferred_element_type=F32
+                )
+            )
+    top = functools.reduce(jnp.maximum, tops)
+    factors = [jnp.exp2(t - top) for t in tops]
+    denominator = functools.reduce(jnp.add, [f * d for f, d in zip(factors, denominators)])
+    total = functools.reduce(jnp.add, [f * w for f, w in zip(factors, weighted)])
+    part_out[:, :, 0:LAT] = (total / denominator).astype(BF16).reshape(X, ROWS, LAT)
+    part_out[:, :, LAT:] = stat_tile(top + jnp.log2(denominator), count).reshape(X, ROWS, 128)
+    for dx in farthest_first(X):
+        send(2, part_out.at[dx], part_in.at[dx], in_group(X - dx, 0))
+    wait_all(send_sem, 1, all_q)
+    pltpu.make_async_copy(sibling_cache, sibling_cache, send_sem.at[7]).wait()
 
     loads[3].wait()
-    for copy in back:
-        copy.wait_recv()
+    wait_all(recv_sem, 2, part_in)
     held = [part_out[0]] + [part_in[dx] for dx in range(1, X)]
     total, stat = combine(
         [part[:, 0:LAT].astype(F32) for part in held], [read_stat(part[:, LAT:]) for part in held]
@@ -269,17 +279,16 @@
     )
     own_out[...] = dot(gather, stacked).astype(BF16).reshape(Y, 32, 128)
 
-    sent = [send(3, d, own_out.at[d], own_in.at[d], along_y(Y - d)) for d in farthest_first(Y)]
-    for copy in back:
-        copy.wait_send()
+    for d in farthest_first(Y):
+        send(3, own_out.at[d], own_in.at[d], along_y(Y - d))
+    wait_all(send_sem, 2, part_in)
     r = iota((128, 16), 0)
     k = iota((128, 16), 1)
     to_row = r & 15
     block = r >> 4
     source = (block & 3) * 4 + (block >> 2) * 2 + (to_row & 1)
     pick = one_where(k == source)
-    for copy in sent:
-        copy.wait_recv()
+    wait_all(recv_sem, 3, own_in)
     held = [own_out[0]] + [own_in[d] for d in range(1, Y)]
     latent_out, _ = combine(
         [part[0:16].astype(F32) for part in held], [read_stat(part[16:32]) for part in held]
@@ -289,57 +298,40 @@
         wide = jnp.concatenate([picked[64 * h + 16 * c : 64 * h + 16 * (c + 1)] for c in range(4)], axis=1)
         heads[0, :, DV * h : DV * (h + 1)] = dot(wide, value_lift[h])[0:2].astype(BF16).astype(F32)
 
-    last = sent
-    sent = [send(4, d, heads.at[0], heads.at[d], along_z(d)) for d in farthest_first(Z)]
-    for copy in last:
-        copy.wait_send()
-    for copy in sent:
-        copy.wait_recv()
+    for d in farthest_first(Z):
+        send(4, heads.at[0], heads.at[d], along_z(d))
+    wait_all(send_sem, 3, own_in)
+    wait_all(recv_sem, 4, heads)
     every = jnp.concatenate([heads[d] for d in range(Z)], axis=0).astype(BF16)
     product = dot(every, placed[...])
     for g in range(G):
-        sums_out[g] = product[:, 128 * g : 128 * (g + 1)]
-
-    last = sent
-    sent = []
-    for g in sorted(range(1, G), key=lambda g: -min(AWAY[g][0], X - AWAY[g][0])):
+        for half in range(2):
+            tile = product[8 * half : 8 * half + 8, 128 * g : 128 * (g + 1)]
+            sums_out[g, :, half, :] = blocks_transposed(tile)
+
+    plane = [(g, d) for g in range(G) for d in range(Y)][1:]
+    distance = lambda at: min(AWAY[at[0]][0], X - AWAY[at[0]][0]) + min(at[1], Y - at[1])
+    for g, d in sorted(plane, key=lambda at: -distance(at)):
         dx, dc = AWAY[g]
-        chunk = ((x + dx) & (X - 1)) * 2 + ((core + dc) & 1)
-        sent.append(send(5, g, sums_out.at[chunk], sums_in.at[g], in_group(dx, dc)))
-    for copy in last:
-        copy.wait_send()
-    for copy in sent:
-        copy.wait_recv()
-    total = functools.reduce(jnp.add, [sums_in[g] for g in range(1, G)]) + sums_out[x * 2 + core]
-
-    came_from = ((iota((8, 128), 1) >> 4) - iota((8, 128), 0)) & 7
-    for half in range(2):
-        turned = pltpu.roll(total[8 * half : 8 * half + 8], 0, 1, stride=16, stride_axis=0)
-        for d in range(Y):
-            line = jnp.sum(jnp.where(came_from == d, turned, 0.0), axis=0, keepdims=True)
-            last_out[d, half : half + 1, :] = pltpu.roll(line, (128 - 16 * d) & 127, 1)
-    last = sent
-    sent = [send(6, d, last_out.at[d], last_in.at[d], along_y(d)) for d in farthest_first(Y)]
-    for copy in last:
-        copy.wait_send()
-    for copy in sent:
-        copy.wait_recv()
-    total = functools.reduce(jnp.add, [last_in[d] for d in range(1, Y)]) + last_out[0]
+        to_x, to_core, to_y = (x + dx) & (X - 1), (core + dc) & 1, (y + d) & (Y - 1)
+        target = (row, (to_x * Y + to_y) * 2 + to_core)
+        send(5, sums_out.at[to_x * 2 + to_core, d], sums_in.at[g * Y + d], target)
+    wait_all(send_sem, 4, heads)
+    wait_all(recv_sem, 5, sums_in)
+    total = functools.reduce(jnp.add, [sums_in[at] for at in range(1, G * Y)]) + sums_out[x * 2 + core, 0]
     for half in range(2):
         wide = jnp.broadcast_to(total[half : half + 1], (8, 128))
         wide = pltpu.roll(wide, 16, 1, stride=16, stride_axis=0)
         for at in range(8):
             sequence = (row - (4 * half + at // 2)) & (Z - 1)
             out[sequence, at % 2 : at % 2 + 1, :] = wide[7 - at : 8 - at, 0:COLS]
-    for copy in sent:
-        copy.wait_send()
+    wait_all(send_sem, 5, sums_in)
 
 
 def on_device(nope_query, rope_query, key_lift, value_lift, out_weight, latent_cache, lengths):
     cache = latent_cache[0].T
     in_hbm = (nope_query, rope_query, key_lift, value_lift, out_weight, cache)
     span = cache.shape[1]
-    most = max(G, Y)
     vmem = pl.BlockSpec(memory_space=pltpu.VMEM)
     hbm = pl.BlockSpec(memory_space=pltpu.HBM)
     return pl.pallas_call(
@@ -362,13 +354,11 @@
             pltpu.VMEM((Y, 32, 128), BF16),
             pltpu.VMEM((Y, 32, 128), BF16),
             pltpu.VMEM((Z, 2, 2 * DV), F32),
-            pltpu.VMEM((G, 16, 128), F32),
-            pltpu.VMEM((G, 16, 128), F32),
-            pltpu.VMEM((Y, 2, 128), F32),
-            pltpu.VMEM((Y, 2, 128), F32),
+            pltpu.VMEM((G, Y, 2, 128), F32),
+            pltpu.VMEM((G * Y, 2, 128), F32),
             pltpu.SemaphoreType.DMA((6,)),
-            pltpu.SemaphoreType.DMA((7, most)),
-            pltpu.SemaphoreType.DMA((7, most)),
+            pltpu.SemaphoreType.DMA((8,)),
+            pltpu.SemaphoreType.DMA((8,)),
         ],
         compiler_params=pltpu.CompilerParams(
             collective_id=0, has_side_effects=True, vmem_limit_bytes=32 << 20

time: 49.7 us -> 47.7 us (0.960)
  Pallas kernels: 48.3 us -> 46.3 us
    pallas_call x1, Pallas kernels: 48.3 us -> 46.3 us  [on_device(): pl.pallas_call(kernel, out_shape=jax.ShapeDtypeStruct((Z, 2, COLS), F32),...]
where the time goes in v2:
time: 47.7 us; the launch traced here: 47.6 us
  Pallas kernels  46.3 us (97%)
  between operations  0.66 us (1%)
  local copies, waits for them, and re-layouts  0.6 us (1%)
    pallas_call x1, Pallas kernels, on_device(): pl.pallas_call(kernel, out_shape=jax.ShapeDtypeStruct((Z, 2, COLS), F32),...  46.3 us

profile of v2, /device:TPU:1, one launch (start us, length us, event | category | flops | bytes accessed | tf_op | source)
XLA Modules:
  0.0 47.6 jit_solution(15140698402221227359)
XLA Ops:
  0.7 46.3 %shard_map.73 = f32[8,2,14]{2,1,0:T(2,128)S(1)} custom-call(s32[1]{0:T(128)S(6)} %copy.9.lengths, bf16[1,2,2,128]{3,2,1,0:T(2,128)(2,1)} %nope_hbm.1, bf16[1,2,2,64]{3,2,1,0:T(2,128)(2,1)} %rope_hbm.1, bf16[2,128,512]{2,1,0:T(8,128)(2,1)} %key_lift_hbm.1, bf16[2,512,128]{2,1,0:T(8,128)(2,1)} %value_lift_hbm.1, bf16[256,896]{1,0:T(8,128)(2,1)} %weight_hbm.1, ...), custom_call_target="tpu_custom_call" | custom-call | flops 600000000 | bytes 2500000 | tf_op jit(solution)/shard_map/pallas_call | solution.py:337
  47.0 0.6 %copy.10 = f32[8,2,14]{2,1,0:T(2,128)} copy(f32[8,2,14]{2,1,0:T(2,128)S(1)} %shard_map.73) | data formatting | bytes 1792

commit v3 on v2

--- a/solution.py
+++ b/solution.py
@@ -22,8 +22,8 @@
 BF16 = jnp.bfloat16
 
 AWAY = [(dx, dc) for dx in range(X) for dc in range(2)]
-ROWS = 4 * Y
-ROWS_BITS = ROWS.bit_length() - 1
+SAME = [(dx, dy) for dx in range(X) for dy in range(Y)]
+N = len(SAME)
 
 
 def iota(shape, axis):
@@ -34,8 +34,12 @@
     return jnp.dot(a, b, preferred_element_type=F32)
 
 
+def hops(d, n):
+    return min(d, n - d)
+
+
 def farthest_first(n):
-    return sorted(range(1, n), key=lambda d: -min(d, n - d))
+    return sorted(range(1, n), key=lambda d: -hops(d, n))
 
 
 def one_where(condition):
@@ -48,21 +52,6 @@
     middle = rest.astype(BF16)
     low = (rest - middle.astype(F32)).astype(BF16)
     return high, middle, low
-
-
-def stat_tile(value, rows):
-    high, middle, low = split_three(jnp.broadcast_to(value, (rows, 128)))
-    lane = iota((rows, 128), 1)
-    tile = jnp.where(
-        lane == 0,
-        high.astype(F32),
-        jnp.where(lane == 1, middle.astype(F32), jnp.where(lane == 2, low.astype(F32), 0.0)),
-    )
-    return tile.astype(BF16)
-
-
-def read_stat(tile):
-    return jnp.sum(tile.astype(F32), axis=1, keepdims=True)
 
 
 def blocks_transposed(tile):
@@ -73,14 +62,6 @@
         stays = (row & step) == (block & step)
         tile = jnp.where(stays, tile, jnp.where((row & step) == 0, above, below))
     return tile
-
-
-def combine(parts, stats):
-    top = functools.reduce(jnp.maximum, stats)
-    factors = [jnp.exp2(stat - top) for stat in stats]
-    weight = functools.reduce(jnp.add, factors)
-    total = functools.reduce(jnp.add, [f * p for f, p in zip(factors, parts)])
-    return total / weight, top + jnp.log2(weight)
 
 
 def kernel(
@@ -99,12 +80,12 @@
     weight,
     cache,
     placed,
-    near_q,
-    all_q,
+    latents,
+    rotaries,
     part_out,
     part_in,
-    own_out,
-    own_in,
+    stat_out,
+    stat_in,
     heads,
     sums_out,
     sums_in,
@@ -118,11 +99,9 @@
     y = (ctx >> 1) & (Y - 1)
     x = ctx >> Y.bit_length()
 
-    def along_y(d):
-        return (row, (x * Y + ((y + d) & (Y - 1))) * 2 + core)
-
-    def in_group(dx, dc):
-        return (row, (((x + dx) & (X - 1)) * Y + y) * 2 + ((core + dc) & 1))
+    def in_plane(dx, dy, dc=0):
+        to_x, to_y, to_core = (x + dx) & (X - 1), (y + dy) & (Y - 1), (core + dc) & 1
+        return (row, (to_x * Y + to_y) * 2 + to_core)
 
     def along_z(d):
         return ((row + d) & (Z - 1), ctx)
@@ -139,10 +118,11 @@
         loads[at].start()
 
     barrier = pltpu.get_barrier_semaphore()
+    far = sorted(range(1, N), key=lambda at: -hops(SAME[at][0], X) - hops(SAME[at][1], Y))
     partners = (
-        [in_group(*away) for away in AWAY[1:]]
-        + [along_y(d) for d in range(1, Y)]
-        + [along_z(d) for d in range(1, Z)]
+        [in_plane(*SAME[at]) for at in far]
+        + [along_z(d) for d in farthest_first(Z)]
+        + [in_plane(0, 0, 1)]
     )
     for partner in partners:
         pl.semaphore_signal(barrier, inc=1, device_id=partner, device_id_type=MESH)
@@ -169,8 +149,9 @@
         loads[at].wait()
     nope_rows = nope[0].astype(F32)
     rope_rows = rope[0].astype(F32)
+    for j in range(2):
+        rotaries[0, j : j + 1, :] = jnp.concatenate([rope_rows[j, h : h + 1, :] for h in range(2)], axis=1)
     latent = jnp.zeros((16, 128), F32)
-    rotary = jnp.zeros((16, DR), F32)
     for h in range(2):
         left = jnp.where(
             even,
@@ -182,40 +163,18 @@
             latent = jnp.where(
                 (row16 >> 1) == 2 * c + h, lifted[:, 128 * c : 128 * (c + 1)], latent
             )
-        for j in range(2):
-            rotary = jnp.where(
-                row16[:, :DR] == 2 * h + j,
-                jnp.broadcast_to(rope_rows[j, h : h + 1, :], (16, DR)),
-                rotary,
-            )
-    near_q[0, 0:16, :] = latent.astype(BF16)
-    near_q[0, 16:32, :] = jnp.concatenate([rotary, jnp.zeros((16, 128 - DR), F32)], axis=1).astype(BF16)
+    latents[0] = latent.astype(BF16)
     for part in range(2):
         cache[part, LAT + DR :, :] = jnp.zeros((128 - DR, cache.shape[2]), BF16)
 
     pl.semaphore_wait(barrier, len(partners))
 
-    for d in farthest_first(Y):
-        send(0, near_q.at[0], near_q.at[d], along_y(d))
+    for at in far:
+        device = in_plane(*SAME[at])
+        send(0, latents.at[0], latents.at[at], device)
+        send(1, rotaries.at[0], rotaries.at[at], device)
     sibling_cache = cache.at[1, pl.ds(0, LAT + DR)]
-    send(7, cache_hbm, sibling_cache, in_group(0, 1))
-
-    r = iota((5 * ROWS, Y * 32), 0)
-    k = iota((5 * ROWS, Y * 32), 1)
-    i = r & (ROWS - 1)
-    spread = one_where(k == (i >> 2) * 32 + (r >> ROWS_BITS) * 4 + (i & 3))
-    r = iota((Y * 32, 5 * ROWS), 0)
-    k = iota((Y * 32, 5 * ROWS), 1)
-    place = r & 31
-    gather = one_where(k == jnp.minimum(place >> 2, 4) * ROWS + (r >> 5) * 4 + (place & 3))
-    wait_all(recv_sem, 0, near_q)
-    rows = dot(spread, near_q[...].reshape(Y * 32, 128))
-    for c in range(5):
-        all_q[0, :, 128 * c : 128 * (c + 1)] = rows[ROWS * c : ROWS * (c + 1)].astype(BF16)
-
-    for dx in farthest_first(X):
-        send(1, all_q.at[0], all_q.at[dx], in_group(dx, 0))
-    wait_all(send_sem, 0, near_q)
+    send(2, cache_hbm, sibling_cache, in_plane(0, 0, 1))
 
     loads[2].wait()
     span = Y * 2 * COLS
@@ -230,18 +189,32 @@
         choose = one_where(n == source)
         placed[:, 256 * ax : 256 * (ax + 1)] = dot(weight[:, low:high], choose).astype(BF16)
 
+    r, k = iota((128, 128), 0), iota((128, 128), 1)
+    spread = one_where(k == ((r >> 2) & 7) * 16 + (r >> 5) * 4 + (r & 3))
+    gather = one_where(r == ((k >> 2) & 7) * 16 + (k >> 5) * 4 + (k & 3))
+    turn = one_where(iota((4 * N, 2 * N), 1) == (iota((4 * N, 2 * N), 0) >> 2) * 2 + (iota((4 * N, 2 * N), 0) & 1))
+    by_slot = one_where(iota((N, 4 * N), 0) == iota((N, 4 * N), 1) >> 2)
+
     loads[1].wait()
     span = cache.shape[2]
     block = span // 2
-    count = ROWS * X
+    count = 4 * N
     limit = lengths[0] - 1 + (iota((count, 1), 0) & 1)
     scale = LOG2E * (DN + DR) ** -0.5
-    wait_all(recv_sem, 1, all_q)
-    query = all_q[...].reshape(count, LAT + 128)
+    wait_all(recv_sem, 0, latents)
+    wait_all(recv_sem, 1, rotaries)
+    pieces = [dot(spread, latents[8 * at : 8 * at + 8].reshape(128, 128)).astype(BF16) for at in range(N // 8)]
+    pieces = [
+        jnp.concatenate([piece[32 * c : 32 * (c + 1)] for piece in pieces], axis=0) for c in range(4)
+    ]
+    turned = dot(turn, rotaries[...].reshape(2 * N, 128).astype(BF16))
+    second_head = (iota((count, 1), 0) & 2) > 0
+    pieces.append(jnp.where(second_head, pltpu.roll(turned, DR, 1), turned).astype(BF16))
+    query = jnp.concatenate(pieces, axis=1)
     tops, denominators, weighted = [], [], []
     for part in range(2):
         if part:
-            pltpu.make_async_copy(sibling_cache, sibling_cache, recv_sem.at[7]).wait()
+            pltpu.make_async_copy(sibling_cache, sibling_cache, recv_sem.at[2]).wait()
         owner = ctx if part == 0 else ctx + 1 - 2 * core
         for start in range(0, span, block):
             visible = iota((1, block), 1) + (owner * span + start) < limit
@@ -260,38 +233,39 @@
     factors = [jnp.exp2(t - top) for t in tops]
     denominator = functools.reduce(jnp.add, [f * d for f, d in zip(factors, denominators)])
     total = functools.reduce(jnp.add, [f * w for f, w in zip(factors, weighted)])
-    part_out[:, :, 0:LAT] = (total / denominator).astype(BF16).reshape(X, ROWS, LAT)
-    part_out[:, :, LAT:] = stat_tile(top + jnp.log2(denominator), count).reshape(X, ROWS, 128)
-    for dx in farthest_first(X):
-        send(2, part_out.at[dx], part_in.at[dx], in_group(X - dx, 0))
-    wait_all(send_sem, 1, all_q)
-    pltpu.make_async_copy(sibling_cache, sibling_cache, send_sem.at[7]).wait()
-
+    total = (total / denominator).astype(BF16)
+    for at in range(N // 8):
+        rows = total[32 * at : 32 * at + 32]
+        rows = jnp.concatenate([rows[:, 128 * c : 128 * (c + 1)] for c in range(4)], axis=0)
+        part_out[8 * at : 8 * at + 8] = dot(gather, rows).astype(BF16).reshape(8, 16, 128)
+    k, lane = iota((count, 128), 0), iota((count, 128), 1)
+    stat = jnp.where((k & 3) == (lane & 3), top + jnp.log2(denominator), 0.0)
+    stat_out[:, 0, :] = functools.reduce(jnp.add, [dot(by_slot, piece) for piece in split_three(stat)])
+
+    for at in far:
+        dx, dy = SAME[at]
+        device = in_plane(X - dx, Y - dy)
+        send(6, stat_out.at[at], stat_in.at[at], device)
+        send(3, part_out.at[at], part_in.at[at], device)
+    part_in[0] = part_out[0]
+    stat_in[0] = stat_out[0]
+    wait_all(send_sem, 0, latents)
+    wait_all(send_sem, 1, rotaries)
+    pltpu.make_async_copy(sibling_cache, sibling_cache, send_sem.at[2]).wait()
     loads[3].wait()
-    wait_all(recv_sem, 2, part_in)
-    held = [part_out[0]] + [part_in[dx] for dx in range(1, X)]
-    total, stat = combine(
-        [part[:, 0:LAT].astype(F32) for part in held], [read_stat(part[:, LAT:]) for part in held]
-    )
-    total = total.astype(BF16)
-    stacked = jnp.concatenate(
-        [total[:, 128 * c : 128 * (c + 1)] for c in range(4)] + [stat_tile(stat, ROWS)], axis=0
-    )
-    own_out[...] = dot(gather, stacked).astype(BF16).reshape(Y, 32, 128)
-
-    for d in farthest_first(Y):
-        send(3, own_out.at[d], own_in.at[d], along_y(Y - d))
-    wait_all(send_sem, 2, part_in)
     r = iota((128, 16), 0)
     k = iota((128, 16), 1)
     to_row = r & 15
     block = r >> 4
     source = (block & 3) * 4 + (block >> 2) * 2 + (to_row & 1)
     pick = one_where(k == source)
-    wait_all(recv_sem, 3, own_in)
-    held = [own_out[0]] + [own_in[d] for d in range(1, Y)]
-    latent_out, _ = combine(
-        [part[0:16].astype(F32) for part in held], [read_stat(part[16:32]) for part in held]
+    wait_all(recv_sem, 6, stat_in)
+    stat = stat_in[:, 0, :]
+    factor = jnp.exp2(stat - jnp.max(stat, axis=0, keepdims=True))
+    factor = (factor / jnp.sum(factor, axis=0, keepdims=True)).T[0:16]
+    wait_all(recv_sem, 3, part_in)
+    latent_out = functools.reduce(
+        jnp.add, [factor[:, at : at + 1] * part_in[at].astype(F32) for at in range(N)]
     )
     picked = dot(pick, latent_out.astype(BF16)).astype(BF16)
     for h in range(2):
@@ -300,7 +274,8 @@
 
     for d in farthest_first(Z):
         send(4, heads.at[0], heads.at[d], along_z(d))
-    wait_all(send_sem, 3, own_in)
+    wait_all(send_sem, 3, part_in)
+    wait_all(send_sem, 6, stat_in)
     wait_all(recv_sem, 4, heads)
     every = jnp.concatenate([heads[d] for d in range(Z)], axis=0).astype(BF16)
     product = dot(every, placed[...])
@@ -310,12 +285,10 @@
             sums_out[g, :, half, :] = blocks_transposed(tile)
 
     plane = [(g, d) for g in range(G) for d in range(Y)][1:]
-    distance = lambda at: min(AWAY[at[0]][0], X - AWAY[at[0]][0]) + min(at[1], Y - at[1])
-    for g, d in sorted(plane, key=lambda at: -distance(at)):
+    for g, d in sorted(plane, key=lambda at: -hops(AWAY[at[0]][0], X) - hops(at[1], Y)):
         dx, dc = AWAY[g]
-        to_x, to_core, to_y = (x + dx) & (X - 1), (core + dc) & 1, (y + d) & (Y - 1)
-        target = (row, (to_x * Y + to_y) * 2 + to_core)
-        send(5, sums_out.at[to_x * 2 + to_core, d], sums_in.at[g * Y + d], target)
+        chunk = ((x + dx) & (X - 1)) * 2 + ((core + dc) & 1)
+        send(5, sums_out.at[chunk, d], sums_in.at[g * Y + d], in_plane(dx, d, dc))
     wait_all(send_sem, 4, heads)
     wait_all(recv_sem, 5, sums_in)
     total = functools.reduce(jnp.add, [sums_in[at] for at in range(1, G * Y)]) + sums_out[x * 2 + core, 0]
@@ -347,18 +320,18 @@
             pltpu.VMEM(out_weight.shape, BF16),
             pltpu.VMEM((2, LAT + 128, span), BF16),
             pltpu.VMEM((2 * DV, 128 * G), BF16),
-            pltpu.VMEM((Y, 32, 128), BF16),
-            pltpu.VMEM((X, ROWS, LAT + 128), BF16),
-            pltpu.VMEM((X, ROWS, LAT + 128), BF16),
-            pltpu.VMEM((X, ROWS, LAT + 128), BF16),
-            pltpu.VMEM((Y, 32, 128), BF16),
-            pltpu.VMEM((Y, 32, 128), BF16),
+            pltpu.VMEM((N, 16, 128), BF16),
+            pltpu.VMEM((N, 2, 128), F32),
+            pltpu.VMEM((N, 16, 128), BF16),
+            pltpu.VMEM((N, 16, 128), BF16),
+            pltpu.VMEM((N, 1, 128), F32),
+            pltpu.VMEM((N, 1, 128), F32),
             pltpu.VMEM((Z, 2, 2 * DV), F32),
             pltpu.VMEM((G, Y, 2, 128), F32),
             pltpu.VMEM((G * Y, 2, 128), F32),
             pltpu.SemaphoreType.DMA((6,)),
-            pltpu.SemaphoreType.DMA((8,)),
-            pltpu.SemaphoreType.DMA((8,)),
+            pltpu.SemaphoreType.DMA((7,)),
+            pltpu.SemaphoreType.DMA((7,)),
         ],
         compiler_params=pltpu.CompilerParams(
             collective_id=0, has_side_effects=True, vmem_limit_bytes=32 << 20

time: 47.7 us -> 43.5 us (0.912)
  Pallas kernels: 46.3 us -> 42.1 us
    pallas_call x1, Pallas kernels: 46.3 us -> 42.1 us  [on_device(): pl.pallas_call(kernel, out_shape=jax.ShapeDtypeStruct((Z, 2, COLS), F32),...]
where the time goes in v3:
time: 43.5 us; the launch traced here: 43.3 us
  Pallas kernels  42.1 us (97%)
  between operations  0.66 us (2%)
  local copies, waits for them, and re-layouts  0.6 us (1%)
    pallas_call x1, Pallas kernels, on_device(): pl.pallas_call(kernel, out_shape=jax.ShapeDtypeStruct((Z, 2, COLS), F32),...  42.1 us

profile of v3, /device:TPU:1, one launch (start us, length us, event | category | flops | bytes accessed | tf_op | source)
XLA Modules:
  0.0 43.3 jit_solution(17818089062100996809)
XLA Ops:
  0.7 42.1 %shard_map.73 = f32[8,2,14]{2,1,0:T(2,128)S(1)} custom-call(s32[1]{0:T(128)S(6)} %copy.9.lengths, bf16[1,2,2,128]{3,2,1,0:T(2,128)(2,1)} %nope_hbm.1, bf16[1,2,2,64]{3,2,1,0:T(2,128)(2,1)} %rope_hbm.1, bf16[2,128,512]{2,1,0:T(8,128)(2,1)} %key_lift_hbm.1, bf16[2,512,128]{2,1,0:T(8,128)(2,1)} %value_lift_hbm.1, bf16[256,896]{1,0:T(8,128)(2,1)} %weight_hbm.1, ...), custom_call_target="tpu_custom_call" | custom-call | flops 600000000 | bytes 2500000 | tf_op jit(solution)/shard_map/pallas_call | solution.py:310
  42.7 0.6 %copy.10 = f32[8,2,14]{2,1,0:T(2,128)} copy(f32[8,2,14]{2,1,0:T(2,128)S(1)} %shard_map.73) | data formatting | bytes 1792

commit v4 on v3

--- a/solution.py
+++ b/solution.py
@@ -201,8 +201,9 @@
     count = 4 * N
     limit = lengths[0] - 1 + (iota((count, 1), 0) & 1)
     scale = LOG2E * (DN + DR) ** -0.5
+    pltpu.make_async_copy(sibling_cache, sibling_cache, recv_sem.at[2]).wait()
+    wait_all(recv_sem, 1, rotaries)
     wait_all(recv_sem, 0, latents)
-    wait_all(recv_sem, 1, rotaries)
     pieces = [dot(spread, latents[8 * at : 8 * at + 8].reshape(128, 128)).astype(BF16) for at in range(N // 8)]
     pieces = [
         jnp.concatenate([piece[32 * c : 32 * (c + 1)] for piece in pieces], axis=0) for c in range(4)
@@ -213,8 +214,6 @@
     query = jnp.concatenate(pieces, axis=1)
     tops, denominators, weighted = [], [], []
     for part in range(2):
-        if part:
-            pltpu.make_async_copy(sibling_cache, sibling_cache, recv_sem.at[2]).wait()
         owner = ctx if part == 0 else ctx + 1 - 2 * core
         for start in range(0, span, block):
             visible = iota((1, block), 1) + (owner * span + start) < limit
@@ -233,7 +232,7 @@
     factors = [jnp.exp2(t - top) for t in tops]
     denominator = functools.reduce(jnp.add, [f * d for f, d in zip(factors, denominators)])
     total = functools.reduce(jnp.add, [f * w for f, w in zip(factors, weighted)])
-    total = (total / denominator).astype(BF16)
+    total = (total * (1.0 / denominator)).astype(BF16)
     for at in range(N // 8):
         rows = total[32 * at : 32 * at + 32]
         rows = jnp.concatenate([rows[:, 128 * c : 128 * (c + 1)] for c in range(4)], axis=0)
@@ -253,24 +252,20 @@
     wait_all(send_sem, 1, rotaries)
     pltpu.make_async_copy(sibling_cache, sibling_cache, send_sem.at[2]).wait()
     loads[3].wait()
-    r = iota((128, 16), 0)
-    k = iota((128, 16), 1)
-    to_row = r & 15
-    block = r >> 4
-    source = (block & 3) * 4 + (block >> 2) * 2 + (to_row & 1)
-    pick = one_where(k == source)
     wait_all(recv_sem, 6, stat_in)
     stat = stat_in[:, 0, :]
     factor = jnp.exp2(stat - jnp.max(stat, axis=0, keepdims=True))
-    factor = (factor / jnp.sum(factor, axis=0, keepdims=True)).T[0:16]
+    factor = (factor * (1.0 / jnp.sum(factor, axis=0, keepdims=True))).T[0:16]
     wait_all(recv_sem, 3, part_in)
     latent_out = functools.reduce(
         jnp.add, [factor[:, at : at + 1] * part_in[at].astype(F32) for at in range(N)]
     )
-    picked = dot(pick, latent_out.astype(BF16)).astype(BF16)
+    wide = jnp.concatenate([jnp.where(row16 >> 2 == c, latent_out, 0.0) for c in range(4)], axis=1).astype(BF16)
     for h in range(2):
-        wide = jnp.concatenate([picked[64 * h + 16 * c : 64 * h + 16 * (c + 1)] for c in range(4)], axis=1)
-        heads[0, :, DV * h : DV * (h + 1)] = dot(wide, value_lift[h])[0:2].astype(BF16).astype(F32)
+        lifted = dot(wide, value_lift[h])
+        lifted = lifted + pltpu.roll(lifted, 8, 0)
+        lifted = lifted + pltpu.roll(lifted, 4, 0)
+        heads[0, :, DV * h : DV * (h + 1)] = lifted[2 * h : 2 * h + 2].astype(BF16).astype(F32)
 
     for d in farthest_first(Z):
         send(4, heads.at[0], heads.at[d], along_z(d))

time: 43.5 us -> 43.2 us (level)
  no operation moved by 1% of the time
where the time goes in v4:
time: 43.2 us; the launch traced here: 43.1 us
  Pallas kernels  41.8 us (97%)
  between operations  0.66 us (2%)
  local copies, waits for them, and re-layouts  0.6 us (1%)
    pallas_call x1, Pallas kernels, on_device(): pl.pallas_call(kernel, out_shape=jax.ShapeDtypeStruct((Z, 2, COLS), F32),...  41.8 us

profile of v4, /device:TPU:1, one launch (start us, length us, event | category | flops | bytes accessed | tf_op | source)
XLA Modules:
  0.0 43.1 jit_solution(13979778632783652484)
XLA Ops:
  0.7 41.8 %shard_map.73 = f32[8,2,14]{2,1,0:T(2,128)S(1)} custom-call(s32[1]{0:T(128)S(6)} %copy.9.lengths, bf16[1,2,2,128]{3,2,1,0:T(2,128)(2,1)} %nope_hbm.1, bf16[1,2,2,64]{3,2,1,0:T(2,128)(2,1)} %rope_hbm.1, bf16[2,128,512]{2,1,0:T(8,128)(2,1)} %key_lift_hbm.1, bf16[2,512,128]{2,1,0:T(8,128)(2,1)} %value_lift_hbm.1, bf16[256,896]{1,0:T(8,128)(2,1)} %weight_hbm.1, ...), custom_call_target="tpu_custom_call" | custom-call | flops 600000000 | bytes 2500000 | tf_op jit(solution)/shard_map/pallas_call | solution.py:305
  42.5 0.6 %copy.10 = f32[8,2,14]{2,1,0:T(2,128)} copy(f32[8,2,14]{2,1,0:T(2,128)S(1)} %shard_map.73) | data formatting | bytes 1792

commit v5 on v4

--- a/solution.py
+++ b/solution.py
@@ -169,12 +169,16 @@
 
     pl.semaphore_wait(barrier, len(partners))
 
+    sibling_cache = cache.at[1, pl.ds(0, LAT + DR)]
+    quarter = (LAT + DR) // 4
+    for start in range(0, LAT + DR, quarter):
+        rows = pl.ds(start, quarter)
+        send(2, cache_hbm.at[rows], cache.at[1, rows], in_plane(0, 0, 1))
+
     for at in far:
         device = in_plane(*SAME[at])
         send(0, latents.at[0], latents.at[at], device)
         send(1, rotaries.at[0], rotaries.at[at], device)
-    sibling_cache = cache.at[1, pl.ds(0, LAT + DR)]
-    send(2, cache_hbm, sibling_cache, in_plane(0, 0, 1))
 
     loads[2].wait()
     span = Y * 2 * COLS

time: 43.2 us -> 43.2 us (level)
  no operation moved by 1% of the time
where the time goes in v5:
time: 43.2 us; the launch traced here: 43.1 us
  Pallas kernels  41.8 us (97%)
  between operations  0.66 us (2%)
  local copies, waits for them, and re-layouts  0.6 us (1%)
    pallas_call x1, Pallas kernels, on_device(): pl.pallas_call(kernel, out_shape=jax.ShapeDtypeStruct((Z, 2, COLS), F32),...  41.8 us

profile of v5, /device:TPU:1, one launch (start us, length us, event | category | flops | bytes accessed | tf_op | source)
XLA Modules:
  0.0 43.1 jit_solution(98491947094188570)
XLA Ops:
  0.7 41.8 %shard_map.73 = f32[8,2,14]{2,1,0:T(2,128)S(1)} custom-call(s32[1]{0:T(128)S(6)} %copy.9.lengths, bf16[1,2,2,128]{3,2,1,0:T(2,128)(2,1)} %nope_hbm.1, bf16[1,2,2,64]{3,2,1,0:T(2,128)(2,1)} %rope_hbm.1, bf16[2,128,512]{2,1,0:T(8,128)(2,1)} %key_lift_hbm.1, bf16[2,512,128]{2,1,0:T(8,128)(2,1)} %value_lift_hbm.1, bf16[256,896]{1,0:T(8,128)(2,1)} %weight_hbm.1, ...), custom_call_target="tpu_custom_call" | custom-call | flops 600000000 | bytes 2500000 | tf_op jit(solution)/shard_map/pallas_call | solution.py:309
  42.5 0.6 %copy.10 = f32[8,2,14]{2,1,0:T(2,128)} copy(f32[8,2,14]{2,1,0:T(2,128)S(1)} %shard_map.73) | data formatting | bytes 1792

commit v6 on v5

--- a/solution.py
+++ b/solution.py
@@ -24,6 +24,8 @@
 AWAY = [(dx, dc) for dx in range(X) for dc in range(2)]
 SAME = [(dx, dy) for dx in range(X) for dy in range(Y)]
 N = len(SAME)
+ROWS = 4 * Y
+HALVES = ((2, 3), (1, 0))
 
 
 def iota(shape, axis):
@@ -119,6 +121,7 @@
 
     barrier = pltpu.get_barrier_semaphore()
     far = sorted(range(1, N), key=lambda at: -hops(SAME[at][0], X) - hops(SAME[at][1], Y))
+    halves = [[at for at in far if SAME[at][0] in half] for half in HALVES]
     partners = (
         [in_plane(*SAME[at]) for at in far]
         + [along_z(d) for d in farthest_first(Z)]
@@ -139,8 +142,8 @@
             device_id_type=MESH,
         ).start()
 
-    def wait_all(sems, stage, buffer):
-        slots = buffer.at[pl.ds(1, buffer.shape[0] - 1)]
+    def wait_all(sems, stage, buffer, count=None):
+        slots = buffer.at[pl.ds(1, buffer.shape[0] - 1 if count is None else count)]
         pltpu.make_async_copy(slots, slots, sems.at[stage]).wait()
 
     row16 = iota((16, 128), 0)
@@ -175,10 +178,11 @@
         rows = pl.ds(start, quarter)
         send(2, cache_hbm.at[rows], cache.at[1, rows], in_plane(0, 0, 1))
 
-    for at in far:
-        device = in_plane(*SAME[at])
-        send(0, latents.at[0], latents.at[at], device)
-        send(1, rotaries.at[0], rotaries.at[at], device)
+    for half, slots in enumerate(halves):
+        for at in slots:
+            device = in_plane(*SAME[at])
+            send(7 + half, latents.at[0], latents.at[at], device)
+            send(half, rotaries.at[0], rotaries.at[at], device)
 
     loads[2].wait()
     span = Y * 2 * COLS
@@ -193,67 +197,71 @@
         choose = one_where(n == source)
         placed[:, 256 * ax : 256 * (ax + 1)] = dot(weight[:, low:high], choose).astype(BF16)
 
+    count = 2 * ROWS
     r, k = iota((128, 128), 0), iota((128, 128), 1)
     spread = one_where(k == ((r >> 2) & 7) * 16 + (r >> 5) * 4 + (r & 3))
     gather = one_where(r == ((k >> 2) & 7) * 16 + (k >> 5) * 4 + (k & 3))
-    turn = one_where(iota((4 * N, 2 * N), 1) == (iota((4 * N, 2 * N), 0) >> 2) * 2 + (iota((4 * N, 2 * N), 0) & 1))
-    by_slot = one_where(iota((N, 4 * N), 0) == iota((N, 4 * N), 1) >> 2)
+    r, k = iota((ROWS, 2 * Y), 0), iota((ROWS, 2 * Y), 1)
+    turn = one_where(k == (r >> 2) * 2 + (r & 1))
+    second_head = (iota((ROWS, 1), 0) & 2) > 0
+    r, k = iota((2 * Y, count), 0), iota((2 * Y, count), 1)
+    by_slot = one_where(r == k >> 2)
 
     loads[1].wait()
     span = cache.shape[2]
-    block = span // 2
-    count = 4 * N
     limit = lengths[0] - 1 + (iota((count, 1), 0) & 1)
     scale = LOG2E * (DN + DR) ** -0.5
     pltpu.make_async_copy(sibling_cache, sibling_cache, recv_sem.at[2]).wait()
-    wait_all(recv_sem, 1, rotaries)
-    wait_all(recv_sem, 0, latents)
-    pieces = [dot(spread, latents[8 * at : 8 * at + 8].reshape(128, 128)).astype(BF16) for at in range(N // 8)]
-    pieces = [
-        jnp.concatenate([piece[32 * c : 32 * (c + 1)] for piece in pieces], axis=0) for c in range(4)
-    ]
-    turned = dot(turn, rotaries[...].reshape(2 * N, 128).astype(BF16))
-    second_head = (iota((count, 1), 0) & 2) > 0
-    pieces.append(jnp.where(second_head, pltpu.roll(turned, DR, 1), turned).astype(BF16))
-    query = jnp.concatenate(pieces, axis=1)
-    tops, denominators, weighted = [], [], []
-    for part in range(2):
-        owner = ctx if part == 0 else ctx + 1 - 2 * core
-        for start in range(0, span, block):
-            visible = iota((1, block), 1) + (owner * span + start) < limit
-            keys = cache[part, :, start : start + block]
-            scores = jnp.where(visible, dot(query, keys) * scale, LOWEST)
+    for half, (slots, at_x) in enumerate(zip(halves, HALVES)):
+        wait_all(recv_sem, half, rotaries, len(slots))
+        wait_all(recv_sem, 7 + half, latents, len(slots))
+        query = []
+        for dx in at_x:
+            rows = dot(spread, latents[Y * dx : Y * (dx + 1)].reshape(128, 128)).astype(BF16)
+            rotary = dot(turn, rotaries[Y * dx : Y * (dx + 1)].reshape(2 * Y, 128).astype(BF16))
+            rotary = jnp.where(second_head, pltpu.roll(rotary, DR, 1), rotary).astype(BF16)
+            rows = [rows[ROWS * c : ROWS * (c + 1)] for c in range(4)]
+            query.append(jnp.concatenate(rows + [rotary], axis=1))
+        query = jnp.concatenate(query, axis=0)
+        tops, denominators, weighted = [], [], []
+        for part in range(2):
+            owner = ctx if part == 0 else ctx + 1 - 2 * core
+            visible = iota((1, span), 1) + owner * span < limit
+            scores = jnp.where(visible, dot(query, cache[part]) * scale, LOWEST)
             top = jnp.max(scores, axis=1, keepdims=True)
             expo = jnp.exp2(scores - top)
             tops.append(top)
             denominators.append(jnp.sum(expo, axis=1, keepdims=True))
             weighted.append(
                 lax.dot_general(
-                    expo.astype(BF16), keys[0:LAT], (((1,), (1,)), ((), ())), preferred_element_type=F32
+                    expo.astype(BF16), cache[part, 0:LAT, :], (((1,), (1,)), ((), ())), preferred_element_type=F32
                 )
             )
-    top = functools.reduce(jnp.maximum, tops)
-    factors = [jnp.exp2(t - top) for t in tops]
-    denominator = functools.reduce(jnp.add, [f * d for f, d in zip(factors, denominators)])
-    total = functools.reduce(jnp.add, [f * w for f, w in zip(factors, weighted)])
-    total = (total * (1.0 / denominator)).astype(BF16)
-    for at in range(N // 8):
-        rows = total[32 * at : 32 * at + 32]
-        rows = jnp.concatenate([rows[:, 128 * c : 128 * (c + 1)] for c in range(4)], axis=0)
-        part_out[8 * at : 8 * at + 8] = dot(gather, rows).astype(BF16).reshape(8, 16, 128)
-    k, lane = iota((count, 128), 0), iota((count, 128), 1)
-    stat = jnp.where((k & 3) == (lane & 3), top + jnp.log2(denominator), 0.0)
-    stat_out[:, 0, :] = functools.reduce(jnp.add, [dot(by_slot, piece) for piece in split_three(stat)])
-
-    for at in far:
-        dx, dy = SAME[at]
-        device = in_plane(X - dx, Y - dy)
-        send(6, stat_out.at[at], stat_in.at[at], device)
-        send(3, part_out.at[at], part_in.at[at], device)
+        top = jnp.maximum(tops[0], tops[1])
+        factors = [jnp.exp2(t - top) for t in tops]
+        denominator = factors[0] * denominators[0] + factors[1] * denominators[1]
+        inverse = 1.0 / denominator
+        total = (weighted[0] * (factors[0] * inverse) + weighted[1] * (factors[1] * inverse)).astype(BF16)
+        for at, dx in enumerate(at_x):
+            rows = total[ROWS * at : ROWS * (at + 1)]
+            rows = jnp.concatenate([rows[:, 128 * c : 128 * (c + 1)] for c in range(4)], axis=0)
+            part_out[Y * dx : Y * (dx + 1)] = dot(gather, rows).astype(BF16).reshape(Y, 16, 128)
+        k, lane = iota((count, 128), 0), iota((count, 128), 1)
+        stat = jnp.where((k & 3) == (lane & 3), top + jnp.log2(denominator), 0.0)
+        stat = functools.reduce(jnp.add, [dot(by_slot, piece) for piece in split_three(stat)])
+        for at, dx in enumerate(at_x):
+            stat_out[Y * dx : Y * (dx + 1), 0, :] = stat[Y * at : Y * (at + 1)]
+
+        for at in slots:
+            dx, dy = SAME[at]
+            device = in_plane(X - dx, Y - dy)
+            send(6, stat_out.at[at], stat_in.at[at], device)
+            send(3, part_out.at[at], part_in.at[at], device)
     part_in[0] = part_out[0]
     stat_in[0] = stat_out[0]
-    wait_all(send_sem, 0, latents)
-    wait_all(send_sem, 1, rotaries)
+    for half, slots in enumerate(halves):
+        wait_all(send_sem, half, rotaries, len(slots))
+        wait_all(send_sem, 7 + half, latents, len(slots))
     pltpu.make_async_copy(sibling_cache, sibling_cache, send_sem.at[2]).wait()
     loads[3].wait()
     wait_all(recv_sem, 6, stat_in)
@@ -329,8 +337,8 @@
             pltpu.VMEM((G, Y, 2, 128), F32),
             pltpu.VMEM((G * Y, 2, 128), F32),
             pltpu.SemaphoreType.DMA((6,)),
-            pltpu.SemaphoreType.DMA((7,)),
-            pltpu.SemaphoreType.DMA((7,)),
+            pltpu.SemaphoreType.DMA((9,)),
+            pltpu.SemaphoreType.DMA((9,)),
         ],
         compiler_params=pltpu.CompilerParams(
             collective_id=0, has_side_effects=True, vmem_limit_bytes=32 << 20

time: 43.2 us -> 43.8 us (1.014)
  Pallas kernels: 41.8 us -> 42.4 us
    pallas_call x1, Pallas kernels: 41.8 us -> 42.4 us  [on_device(): pl.pallas_call(kernel, out_shape=jax.ShapeDtypeStruct((Z, 2, COLS), F32),...]
where the time goes in v6:
time: 43.8 us; the launch traced here: 43.7 us
  Pallas kernels  42.4 us (97%)
  between operations  0.66 us (2%)
  local copies, waits for them, and re-layouts  0.6 us (1%)
    pallas_call x1, Pallas kernels, on_device(): pl.pallas_call(kernel, out_shape=jax.ShapeDtypeStruct((Z, 2, COLS), F32),...  42.4 us

profile of v6, /device:TPU:1, one launch (start us, length us, event | category | flops | bytes accessed | tf_op | source)
XLA Modules:
  0.0 43.7 jit_solution(3951573062624610414)
XLA Ops:
  0.7 42.4 %shard_map.73 = f32[8,2,14]{2,1,0:T(2,128)S(1)} custom-call(s32[1]{0:T(128)S(6)} %copy.9.lengths, bf16[1,2,2,128]{3,2,1,0:T(2,128)(2,1)} %nope_hbm.1, bf16[1,2,2,64]{3,2,1,0:T(2,128)(2,1)} %rope_hbm.1, bf16[2,128,512]{2,1,0:T(8,128)(2,1)} %key_lift_hbm.1, bf16[2,512,128]{2,1,0:T(8,128)(2,1)} %value_lift_hbm.1, bf16[256,896]{1,0:T(8,128)(2,1)} %weight_hbm.1, ...), custom_call_target="tpu_custom_call" | custom-call | flops 600000000 | bytes 2500000 | tf_op jit(solution)/shard_map/pallas_call | solution.py:317
  43.1 0.6 %copy.10 = f32[8,2,14]{2,1,0:T(2,128)} copy(f32[8,2,14]{2,1,0:T(2,128)S(1)} %shard_map.73) | data formatting | bytes 1792

commit v7 on v5

--- a/solution.py
+++ b/solution.py
@@ -40,6 +40,10 @@
 
 def farthest_first(n):
     return sorted(range(1, n), key=lambda d: -hops(d, n))
+
+
+def dot_last(a, b):
+    return lax.dot_general(a, b, (((1,), (1,)), ((), ())), preferred_element_type=F32)
 
 
 def one_where(condition):
@@ -195,13 +199,13 @@
 
     r, k = iota((128, 128), 0), iota((128, 128), 1)
     spread = one_where(k == ((r >> 2) & 7) * 16 + (r >> 5) * 4 + (r & 3))
-    gather = one_where(r == ((k >> 2) & 7) * 16 + (k >> 5) * 4 + (k & 3))
+    r, k = iota((16 * N, 16 * N), 0), iota((16 * N, 16 * N), 1)
+    gather = one_where(k == ((r >> 2) & 3) * 4 * N + (r >> 4) * 4 + (r & 3))
     turn = one_where(iota((4 * N, 2 * N), 1) == (iota((4 * N, 2 * N), 0) >> 2) * 2 + (iota((4 * N, 2 * N), 0) & 1))
     by_slot = one_where(iota((N, 4 * N), 0) == iota((N, 4 * N), 1) >> 2)
 
     loads[1].wait()
     span = cache.shape[2]
-    block = span // 2
     count = 4 * N
     limit = lengths[0] - 1 + (iota((count, 1), 0) & 1)
     scale = LOG2E * (DN + DR) ** -0.5
@@ -216,31 +220,20 @@
     second_head = (iota((count, 1), 0) & 2) > 0
     pieces.append(jnp.where(second_head, pltpu.roll(turned, DR, 1), turned).astype(BF16))
     query = jnp.concatenate(pieces, axis=1)
-    tops, denominators, weighted = [], [], []
+    scores = []
     for part in range(2):
         owner = ctx if part == 0 else ctx + 1 - 2 * core
-        for start in range(0, span, block):
-            visible = iota((1, block), 1) + (owner * span + start) < limit
-            keys = cache[part, :, start : start + block]
-            scores = jnp.where(visible, dot(query, keys) * scale, LOWEST)
-            top = jnp.max(scores, axis=1, keepdims=True)
-            expo = jnp.exp2(scores - top)
-            tops.append(top)
-            denominators.append(jnp.sum(expo, axis=1, keepdims=True))
-            weighted.append(
-                lax.dot_general(
-                    expo.astype(BF16), keys[0:LAT], (((1,), (1,)), ((), ())), preferred_element_type=F32
-                )
-            )
-    top = functools.reduce(jnp.maximum, tops)
-    factors = [jnp.exp2(t - top) for t in tops]
-    denominator = functools.reduce(jnp.add, [f * d for f, d in zip(factors, denominators)])
-    total = functools.reduce(jnp.add, [f * w for f, w in zip(factors, weighted)])
-    total = (total * (1.0 / denominator)).astype(BF16)
-    for at in range(N // 8):
-        rows = total[32 * at : 32 * at + 32]
-        rows = jnp.concatenate([rows[:, 128 * c : 128 * (c + 1)] for c in range(4)], axis=0)
-        part_out[8 * at : 8 * at + 8] = dot(gather, rows).astype(BF16).reshape(8, 16, 128)
+        visible = iota((1, span), 1) + owner * span < limit
+        scores.append(jnp.where(visible, dot(query, cache[part]) * scale, LOWEST))
+    top = jnp.max(jnp.maximum(scores[0], scores[1]), axis=1, keepdims=True)
+    expos = [jnp.exp2(score - top) for score in scores]
+    denominator = jnp.sum(expos[0] + expos[1], axis=1, keepdims=True)
+    inverse = 1.0 / denominator
+    turned = functools.reduce(
+        jnp.add, [dot_last(cache[part, 0:LAT, :], (expos[part] * inverse).astype(BF16)) for part in range(2)]
+    ).astype(BF16)
+    rows = jnp.concatenate([turned[128 * c : 128 * (c + 1)] for c in range(4)], axis=1)
+    part_out[...] = dot_last(gather, rows).astype(BF16).reshape(N, 16, 128)
     k, lane = iota((count, 128), 0), iota((count, 128), 1)
     stat = jnp.where((k & 3) == (lane & 3), top + jnp.log2(denominator), 0.0)
     stat_out[:, 0, :] = functools.reduce(jnp.add, [dot(by_slot, piece) for piece in split_three(stat)])

time: 43.2 us -> 43.5 us (level)
  no operation moved by 1% of the time
where the time goes in v7:
time: 43.5 us; the launch traced here: 43.3 us
  Pallas kernels  42.1 us (97%)
  between operations  0.66 us (2%)
  local copies, waits for them, and re-layouts  0.6 us (1%)
    pallas_call x1, Pallas kernels, on_device(): pl.pallas_call(kernel, out_shape=jax.ShapeDtypeStruct((Z, 2, COLS), F32),...  42.1 us

profile of v7, /device:TPU:1, one launch (start us, length us, event | category | flops | bytes accessed | tf_op | source)
XLA Modules:
  0.0 43.3 jit_solution(14618024179179115946)
XLA Ops:
  0.7 42.1 %shard_map.73 = f32[8,2,14]{2,1,0:T(2,128)S(1)} custom-call(s32[1]{0:T(128)S(6)} %copy.9.lengths, bf16[1,2,2,128]{3,2,1,0:T(2,128)(2,1)} %nope_hbm.1, bf16[1,2,2,64]{3,2,1,0:T(2,128)(2,1)} %rope_hbm.1, bf16[2,128,512]{2,1,0:T(8,128)(2,1)} %key_lift_hbm.1, bf16[2,512,128]{2,1,0:T(8,128)(2,1)} %value_lift_hbm.1, bf16[256,896]{1,0:T(8,128)(2,1)} %weight_hbm.1, ...), custom_call_target="tpu_custom_call" | custom-call | flops 600000000 | bytes 2500000 | tf_op jit(solution)/shard_map/pallas_call | solution.py:302
  42.7 0.6 %copy.10 = f32[8,2,14]{2,1,0:T(2,128)} copy(f32[8,2,14]{2,1,0:T(2,128)S(1)} %shard_map.73) | data formatting | bytes 1792

commit v8 on v5

--- a/solution.py
+++ b/solution.py
@@ -24,6 +24,7 @@
 AWAY = [(dx, dc) for dx in range(X) for dc in range(2)]
 SAME = [(dx, dy) for dx in range(X) for dy in range(Y)]
 N = len(SAME)
+RELAYED = (4, 3, 5)
 
 
 def iota(shape, axis):
@@ -119,8 +120,9 @@
 
     barrier = pltpu.get_barrier_semaphore()
     far = sorted(range(1, N), key=lambda at: -hops(SAME[at][0], X) - hops(SAME[at][1], Y))
+    direct = [at for at in far if SAME[at][0] == 0 or SAME[at][1] not in RELAYED]
     partners = (
-        [in_plane(*SAME[at]) for at in far]
+        [in_plane(*SAME[at]) for at in direct]
         + [along_z(d) for d in farthest_first(Z)]
         + [in_plane(0, 0, 1)]
     )
@@ -139,8 +141,8 @@
             device_id_type=MESH,
         ).start()
 
-    def wait_all(sems, stage, buffer):
-        slots = buffer.at[pl.ds(1, buffer.shape[0] - 1)]
+    def wait_all(sems, stage, buffer, count=None):
+        slots = buffer.at[pl.ds(1, buffer.shape[0] - 1 if count is None else count)]
         pltpu.make_async_copy(slots, slots, sems.at[stage]).wait()
 
     row16 = iota((16, 128), 0)
@@ -175,10 +177,21 @@
         rows = pl.ds(start, quarter)
         send(2, cache_hbm.at[rows], cache.at[1, rows], in_plane(0, 0, 1))
 
-    for at in far:
-        device = in_plane(*SAME[at])
-        send(0, latents.at[0], latents.at[at], device)
-        send(1, rotaries.at[0], rotaries.at[at], device)
+    for at, dy in enumerate(RELAYED):
+        send(7 + at, latents.at[0], latents.at[dy], in_plane(0, dy))
+        send(10 + at, rotaries.at[0], rotaries.at[dy], in_plane(0, dy))
+    for at in direct:
+        if at not in RELAYED:
+            device = in_plane(*SAME[at])
+            send(0, latents.at[0], latents.at[at], device)
+            send(1, rotaries.at[0], rotaries.at[at], device)
+    for at, dy in enumerate(RELAYED):
+        wait_all(recv_sem, 7 + at, latents, 1)
+        wait_all(recv_sem, 10 + at, rotaries, 1)
+        for dx in farthest_first(X):
+            send(0, latents.at[dy], latents.at[Y * dx + dy], in_plane(dx, 0))
+            send(1, rotaries.at[dy], rotaries.at[Y * dx + dy], in_plane(dx, 0))
+    others = N - 1 - len(RELAYED)
 
     loads[2].wait()
     span = Y * 2 * COLS
@@ -206,8 +219,8 @@
     limit = lengths[0] - 1 + (iota((count, 1), 0) & 1)
     scale = LOG2E * (DN + DR) ** -0.5
     pltpu.make_async_copy(sibling_cache, sibling_cache, recv_sem.at[2]).wait()
-    wait_all(recv_sem, 1, rotaries)
-    wait_all(recv_sem, 0, latents)
+    wait_all(recv_sem, 1, rotaries, others)
+    wait_all(recv_sem, 0, latents, others)
     pieces = [dot(spread, latents[8 * at : 8 * at + 8].reshape(128, 128)).astype(BF16) for at in range(N // 8)]
     pieces = [
         jnp.concatenate([piece[32 * c : 32 * (c + 1)] for piece in pieces], axis=0) for c in range(4)
@@ -252,8 +265,11 @@
         send(3, part_out.at[at], part_in.at[at], device)
     part_in[0] = part_out[0]
     stat_in[0] = stat_out[0]
-    wait_all(send_sem, 0, latents)
-    wait_all(send_sem, 1, rotaries)
+    wait_all(send_sem, 0, latents, others)
+    wait_all(send_sem, 1, rotaries, others)
+    for at in range(len(RELAYED)):
+        wait_all(send_sem, 7 + at, latents, 1)
+        wait_all(send_sem, 10 + at, rotaries, 1)
     pltpu.make_async_copy(sibling_cache, sibling_cache, send_sem.at[2]).wait()
     loads[3].wait()
     wait_all(recv_sem, 6, stat_in)
@@ -329,8 +345,8 @@
             pltpu.VMEM((G, Y, 2, 128), F32),
             pltpu.VMEM((G * Y, 2, 128), F32),
             pltpu.SemaphoreType.DMA((6,)),
-            pltpu.SemaphoreType.DMA((7,)),
-            pltpu.SemaphoreType.DMA((7,)),
+            pltpu.SemaphoreType.DMA((13,)),
+            pltpu.SemaphoreType.DMA((13,)),
         ],
         compiler_params=pltpu.CompilerParams(
             collective_id=0, has_side_effects=True, vmem_limit_bytes=32 << 20

time: 43.2 us -> 44.7 us (1.035)
  Pallas kernels: 41.8 us -> 43.3 us
    pallas_call x1, Pallas kernels: 41.8 us -> 43.3 us  [on_device(): pl.pallas_call(kernel, out_shape=jax.ShapeDtypeStruct((Z, 2, COLS), F32),...]
where the time goes in v8:
time: 44.7 us; the launch traced here: 44.6 us
  Pallas kernels  43.3 us (97%)
  between operations  0.66 us (1%)
  local copies, waits for them, and re-layouts  0.6 us (1%)
    pallas_call x1, Pallas kernels, on_device(): pl.pallas_call(kernel, out_shape=jax.ShapeDtypeStruct((Z, 2, COLS), F32),...  43.3 us

profile of v8, /device:TPU:1, one launch (start us, length us, event | category | flops | bytes accessed | tf_op | source)
XLA Modules:
  0.0 44.6 jit_solution(7428097955356457368)
XLA Ops:
  0.7 43.3 %shard_map.73 = f32[8,2,14]{2,1,0:T(2,128)S(1)} custom-call(s32[1]{0:T(128)S(6)} %copy.9.lengths, bf16[1,2,2,128]{3,2,1,0:T(2,128)(2,1)} %nope_hbm.1, bf16[1,2,2,64]{3,2,1,0:T(2,128)(2,1)} %rope_hbm.1, bf16[2,128,512]{2,1,0:T(8,128)(2,1)} %key_lift_hbm.1, bf16[2,512,128]{2,1,0:T(8,128)(2,1)} %value_lift_hbm.1, bf16[256,896]{1,0:T(8,128)(2,1)} %weight_hbm.1, ...), custom_call_target="tpu_custom_call" | custom-call | flops 600000000 | bytes 2500000 | tf_op jit(solution)/shard_map/pallas_call | solution.py:325
  43.9 0.6 %copy.10 = f32[8,2,14]{2,1,0:T(2,128)} copy(f32[8,2,14]{2,1,0:T(2,128)S(1)} %shard_map.73) | data formatting | bytes 1792

commit v9 on v5

--- a/solution.py
+++ b/solution.py
@@ -149,8 +149,8 @@
         loads[at].wait()
     nope_rows = nope[0].astype(F32)
     rope_rows = rope[0].astype(F32)
-    for j in range(2):
-        rotaries[0, j : j + 1, :] = jnp.concatenate([rope_rows[j, h : h + 1, :] for h in range(2)], axis=1)
+    rotary = [jnp.concatenate([rope_rows[j, h : h + 1, :] for h in range(2)], axis=1) for j in range(2)]
+    rotaries[0] = jnp.concatenate(rotary, axis=0).astype(BF16)
     latent = jnp.zeros((16, 128), F32)
     for h in range(2):
         left = jnp.where(
@@ -212,7 +212,7 @@
     pieces = [
         jnp.concatenate([piece[32 * c : 32 * (c + 1)] for piece in pieces], axis=0) for c in range(4)
     ]
-    turned = dot(turn, rotaries[...].reshape(2 * N, 128).astype(BF16))
+    turned = dot(turn, rotaries[...].reshape(2 * N, 128))
     second_head = (iota((count, 1), 0) & 2) > 0
     pieces.append(jnp.where(second_head, pltpu.roll(turned, DR, 1), turned).astype(BF16))
     query = jnp.concatenate(pieces, axis=1)
@@ -279,9 +279,8 @@
     every = jnp.concatenate([heads[d] for d in range(Z)], axis=0).astype(BF16)
     product = dot(every, placed[...])
     for g in range(G):
-        for half in range(2):
-            tile = product[8 * half : 8 * half + 8, 128 * g : 128 * (g + 1)]
-            sums_out[g, :, half, :] = blocks_transposed(tile)
+        tiles = [product[8 * half : 8 * half + 8, 128 * g : 128 * (g + 1)] for half in range(2)]
+        sums_out[g] = jnp.stack([blocks_transposed(tile) for tile in tiles], axis=1).astype(BF16)
 
     plane = [(g, d) for g in range(G) for d in range(Y)][1:]
     for g, d in sorted(plane, key=lambda at: -hops(AWAY[at[0]][0], X) - hops(at[1], Y)):
@@ -290,7 +289,8 @@
         send(5, sums_out.at[chunk, d], sums_in.at[g * Y + d], in_plane(dx, d, dc))
     wait_all(send_sem, 4, heads)
     wait_all(recv_sem, 5, sums_in)
-    total = functools.reduce(jnp.add, [sums_in[at] for at in range(1, G * Y)]) + sums_out[x * 2 + core, 0]
+    sums_in[0] = sums_out[x * 2 + core, 0]
+    total = jnp.sum(sums_in[...].astype(F32), axis=0)
     for half in range(2):
         wide = jnp.broadcast_to(total[half : half + 1], (8, 128))
         wide = pltpu.roll(wide, 16, 1, stride=16, stride_axis=0)
@@ -320,14 +320,14 @@
             pltpu.VMEM((2, LAT + 128, span), BF16),
             pltpu.VMEM((2 * DV, 128 * G), BF16),
             pltpu.VMEM((N, 16, 128), BF16),
-            pltpu.VMEM((N, 2, 128), F32),
+            pltpu.VMEM((N, 2, 128), BF16),
             pltpu.VMEM((N, 16, 128), BF16),
             pltpu.VMEM((N, 16, 128), BF16),
             pltpu.VMEM((N, 1, 128), F32),
             pltpu.VMEM((N, 1, 128), F32),
             pltpu.VMEM((Z, 2, 2 * DV), F32),
-            pltpu.VMEM((G, Y, 2, 128), F32),
-            pltpu.VMEM((G * Y, 2, 128), F32),
+            pltpu.VMEM((G, Y, 2, 128), BF16),
+            pltpu.VMEM((G * Y, 2, 128), BF16),
             pltpu.SemaphoreType.DMA((6,)),
             pltpu.SemaphoreType.DMA((7,)),
             pltpu.SemaphoreType.DMA((7,)),

time: 43.2 us -> 42.4 us (0.981)
  Pallas kernels: 41.8 us -> 41 us
    pallas_call x1, Pallas kernels: 41.8 us -> 41 us  [on_device(): pl.pallas_call(kernel, out_shape=jax.ShapeDtypeStruct((Z, 2, COLS), F32),...]
where the time goes in v9:
time: 42.4 us; the launch traced here: 42.2 us
  Pallas kernels  41 us (97%)
  between operations  0.66 us (2%)
  local copies, waits for them, and re-layouts  0.6 us (1%)
    pallas_call x1, Pallas kernels, on_device(): pl.pallas_call(kernel, out_shape=jax.ShapeDtypeStruct((Z, 2, COLS), F32),...  41 us

profile of v9, /device:TPU:1, one launch (start us, length us, event | category | flops | bytes accessed | tf_op | source)
XLA Modules:
  0.0 42.2 jit_solution(17922864947535467359)
XLA Ops:
  0.7 41.0 %shard_map.73 = f32[8,2,14]{2,1,0:T(2,128)S(1)} custom-call(s32[1]{0:T(128)S(6)} %copy.9.lengths, bf16[1,2,2,128]{3,2,1,0:T(2,128)(2,1)} %nope_hbm.1, bf16[1,2,2,64]{3,2,1,0:T(2,128)(2,1)} %rope_hbm.1, bf16[2,128,512]{2,1,0:T(8,128)(2,1)} %key_lift_hbm.1, bf16[2,512,128]{2,1,0:T(8,128)(2,1)} %value_lift_hbm.1, bf16[256,896]{1,0:T(8,128)(2,1)} %weight_hbm.1, ...), custom_call_target="tpu_custom_call" | custom-call | flops 600000000 | bytes 2500000 | tf_op jit(solution)/shard_map/pallas_call | solution.py:309
  41.6 0.6 %copy.10 = f32[8,2,14]{2,1,0:T(2,128)} copy(f32[8,2,14]{2,1,0:T(2,128)S(1)} %shard_map.73) | data formatting | bytes 1792

commit v10 on v9

--- a/solution.py
+++ b/solution.py
@@ -80,8 +80,7 @@
     weight,
     cache,
     placed,
-    latents,
-    rotaries,
+    queries,
     part_out,
     part_in,
     stat_out,
@@ -150,7 +149,7 @@
     nope_rows = nope[0].astype(F32)
     rope_rows = rope[0].astype(F32)
     rotary = [jnp.concatenate([rope_rows[j, h : h + 1, :] for h in range(2)], axis=1) for j in range(2)]
-    rotaries[0] = jnp.concatenate(rotary, axis=0).astype(BF16)
+    queries[0, 16:18, :] = jnp.concatenate(rotary, axis=0).astype(BF16)
     latent = jnp.zeros((16, 128), F32)
     for h in range(2):
         left = jnp.where(
@@ -163,7 +162,7 @@
             latent = jnp.where(
                 (row16 >> 1) == 2 * c + h, lifted[:, 128 * c : 128 * (c + 1)], latent
             )
-    latents[0] = latent.astype(BF16)
+    queries[0, 0:16, :] = latent.astype(BF16)
     for part in range(2):
         cache[part, LAT + DR :, :] = jnp.zeros((128 - DR, cache.shape[2]), BF16)
 
@@ -176,9 +175,7 @@
         send(2, cache_hbm.at[rows], cache.at[1, rows], in_plane(0, 0, 1))
 
     for at in far:
-        device = in_plane(*SAME[at])
-        send(0, latents.at[0], latents.at[at], device)
-        send(1, rotaries.at[0], rotaries.at[at], device)
+        send(0, queries.at[0], queries.at[at], in_plane(*SAME[at]))
 
     loads[2].wait()
     span = Y * 2 * COLS
@@ -206,13 +203,12 @@
     limit = lengths[0] - 1 + (iota((count, 1), 0) & 1)
     scale = LOG2E * (DN + DR) ** -0.5
     pltpu.make_async_copy(sibling_cache, sibling_cache, recv_sem.at[2]).wait()
-    wait_all(recv_sem, 1, rotaries)
-    wait_all(recv_sem, 0, latents)
-    pieces = [dot(spread, latents[8 * at : 8 * at + 8].reshape(128, 128)).astype(BF16) for at in range(N // 8)]
+    wait_all(recv_sem, 0, queries)
+    pieces = [dot(spread, queries[8 * at : 8 * at + 8, 0:16].reshape(128, 128)).astype(BF16) for at in range(N // 8)]
     pieces = [
         jnp.concatenate([piece[32 * c : 32 * (c + 1)] for piece in pieces], axis=0) for c in range(4)
     ]
-    turned = dot(turn, rotaries[...].reshape(2 * N, 128))
+    turned = dot(turn, queries[:, 16:18].reshape(2 * N, 128))
     second_head = (iota((count, 1), 0) & 2) > 0
     pieces.append(jnp.where(second_head, pltpu.roll(turned, DR, 1), turned).astype(BF16))
     query = jnp.concatenate(pieces, axis=1)
@@ -252,8 +248,7 @@
         send(3, part_out.at[at], part_in.at[at], device)
     part_in[0] = part_out[0]
     stat_in[0] = stat_out[0]
-    wait_all(send_sem, 0, latents)
-    wait_all(send_sem, 1, rotaries)
+    wait_all(send_sem, 0, queries)
     pltpu.make_async_copy(sibling_cache, sibling_cache, send_sem.at[2]).wait()
     loads[3].wait()
     wait_all(recv_sem, 6, stat_in)
@@ -319,8 +314,7 @@
             pltpu.VMEM(out_weight.shape, BF16),
             pltpu.VMEM((2, LAT + 128, span), BF16),
             pltpu.VMEM((2 * DV, 128 * G), BF16),
-            pltpu.VMEM((N, 16, 128), BF16),
-            pltpu.VMEM((N, 2, 128), BF16),
+            pltpu.VMEM((N, 18, 128), BF16),
             pltpu.VMEM((N, 16, 128), BF16),
             pltpu.VMEM((N, 16, 128), BF16),
             pltpu.VMEM((N, 1, 128), F32),

time: 42.4 us -> 43.6 us (1.028)
  Pallas kernels: 41 us -> 42.2 us
    pallas_call x1, Pallas kernels: 41 us -> 42.2 us  [on_device(): pl.pallas_call(kernel, out_shape=jax.ShapeDtypeStruct((Z, 2, COLS), F32),...]
where the time goes in v10:
time: 43.6 us; the launch traced here: 43.5 us
  Pallas kernels  42.2 us (97%)
  between operations  0.66 us (2%)
  local copies, waits for them, and re-layouts  0.6 us (1%)
    pallas_call x1, Pallas kernels, on_device(): pl.pallas_call(kernel, out_shape=jax.ShapeDtypeStruct((Z, 2, COLS), F32),...  42.2 us

profile of v10, /device:TPU:1, one launch (start us, length us, event | category | flops | bytes accessed | tf_op | source)
XLA Modules:
  0.0 43.5 jit_solution(8092047161604669950)
XLA Ops:
  0.7 42.2 %shard_map.73 = f32[8,2,14]{2,1,0:T(2,128)S(1)} custom-call(s32[1]{0:T(128)S(6)} %copy.9.lengths, bf16[1,2,2,128]{3,2,1,0:T(2,128)(2,1)} %nope_hbm.1, bf16[1,2,2,64]{3,2,1,0:T(2,128)(2,1)} %rope_hbm.1, bf16[2,128,512]{2,1,0:T(8,128)(2,1)} %key_lift_hbm.1, bf16[2,512,128]{2,1,0:T(8,128)(2,1)} %value_lift_hbm.1, bf16[256,896]{1,0:T(8,128)(2,1)} %weight_hbm.1, ...), custom_call_target="tpu_custom_call" | custom-call | flops 600000000 | bytes 2500000 | tf_op jit(solution)/shard_map/pallas_call | solution.py:304
  42.9 0.6 %copy.10 = f32[8,2,14]{2,1,0:T(2,128)} copy(f32[8,2,14]{2,1,0:T(2,128)S(1)} %shard_map.73) | data formatting | bytes 1792

commit v11 on v9

--- a/solution.py
+++ b/solution.py
@@ -269,14 +269,14 @@
         lifted = dot(wide, value_lift[h])
         lifted = lifted + pltpu.roll(lifted, 8, 0)
         lifted = lifted + pltpu.roll(lifted, 4, 0)
-        heads[0, :, DV * h : DV * (h + 1)] = lifted[2 * h : 2 * h + 2].astype(BF16).astype(F32)
+        heads[0, :, DV * h : DV * (h + 1)] = lifted[2 * h : 2 * h + 2].astype(BF16)
 
     for d in farthest_first(Z):
         send(4, heads.at[0], heads.at[d], along_z(d))
     wait_all(send_sem, 3, part_in)
     wait_all(send_sem, 6, stat_in)
     wait_all(recv_sem, 4, heads)
-    every = jnp.concatenate([heads[d] for d in range(Z)], axis=0).astype(BF16)
+    every = jnp.concatenate([heads[d].astype(F32) for d in range(Z)], axis=0).astype(BF16)
     product = dot(every, placed[...])
     for g in range(G):
         tiles = [product[8 * half : 8 * half + 8, 128 * g : 128 * (g + 1)] for half in range(2)]
@@ -325,7 +325,7 @@
             pltpu.VMEM((N, 16, 128), BF16),
             pltpu.VMEM((N, 1, 128), F32),
             pltpu.VMEM((N, 1, 128), F32),
-            pltpu.VMEM((Z, 2, 2 * DV), F32),
+            pltpu.VMEM((Z, 2, 2 * DV), BF16),
             pltpu.VMEM((G, Y, 2, 128), BF16),
             pltpu.VMEM((G * Y, 2, 128), BF16),
             pltpu.SemaphoreType.DMA((6,)),

time: 42.4 us -> 42.3 us (level)
  no operation moved by 1% of the time
where the time goes in v11:
time: 42.3 us; the launch traced here: 42.1 us
  Pallas kernels  40.9 us (97%)
  between operations  0.66 us (2%)
  local copies, waits for them, and re-layouts  0.6 us (1%)
    pallas_call x1, Pallas kernels, on_device(): pl.pallas_call(kernel, out_shape=jax.ShapeDtypeStruct((Z, 2, COLS), F32),...  40.9 us

profile of v11, /device:TPU:1, one launch (start us, length us, event | category | flops | bytes accessed | tf_op | source)
XLA Modules:
  0.0 42.1 jit_solution(1312039602768358628)
XLA Ops:
  0.7 40.9 %shard_map.73 = f32[8,2,14]{2,1,0:T(2,128)S(1)} custom-call(s32[1]{0:T(128)S(6)} %copy.9.lengths, bf16[1,2,2,128]{3,2,1,0:T(2,128)(2,1)} %nope_hbm.1, bf16[1,2,2,64]{3,2,1,0:T(2,128)(2,1)} %rope_hbm.1, bf16[2,128,512]{2,1,0:T(8,128)(2,1)} %key_lift_hbm.1, bf16[2,512,128]{2,1,0:T(8,128)(2,1)} %value_lift_hbm.1, bf16[256,896]{1,0:T(8,128)(2,1)} %weight_hbm.1, ...), custom_call_target="tpu_custom_call" | custom-call | flops 600000000 | bytes 2500000 | tf_op jit(solution)/shard_map/pallas_call | solution.py:309
  41.5 0.6 %copy.10 = f32[8,2,14]{2,1,0:T(2,128)} copy(f32[8,2,14]{2,1,0:T(2,128)S(1)} %shard_map.73) | data formatting | bytes 1792
